TPU v7x, 128 devices: a whole 4x4x4 slice. The times are simulated.
128 devices in a mesh: row: 16 (over x, z), grp: 8 (over y, core).
Axes of the slice: x: 4, y: 4, z: 4, core: 2. Of those that a mesh axis runs over, the one named last changes fastest.
Arguments:
- operator_tiles: bfloat16 [1024, 8, 256, 256], P(('row', 'grp')), may hold values from -0.125 to 0.125
- operator_columns: int32 [1024, 8], P(('row', 'grp')), may hold values from 0 to 1023, as said below
- operator_counts: int32 [1024], P(('row', 'grp')), may hold values from 2 to 8, as said below
- prolong_tiles: bfloat16 [1024, 3, 256, 128], P(('row', 'grp')), may hold values from -1.5 to 1.5
- prolong_columns: int32 [1024, 3], P(('row', 'grp')), may hold values from 0 to 255, as said below
- prolong_counts: int32 [1024], P(('row', 'grp')), may hold values from 1 to 3, as said below
Outputs:
- coarse_rows: float32 [256, 128, 1408], P(('row', 'grp'))
Inputs may be any that keep to these rules, and one draw needn't show every extreme that they name: operator_columns[i, 0] = i; every entry lies within 4 panels of i; the live entries of a panel are distinct; entries at slots at or past operator_counts[i] are padding. `operator_counts`: some fine panel has all 8 tiles live. prolong_columns[i, 0] = i // 4; the entries of a panel are distinct and lie within 2 of i // 4. `prolong_counts`: some fine panel has all 3 tiles live.
All inputs are finite; a program needn't handle non-finite values.
Results may differ from a plain program's by a relative error of at most 0.0029.
Values may be sent and summed in bfloat16 or wider, within the bound.
No kernel may reach another device: no remote copies, remote signals or barrier semaphores. Data moves between devices by JAX's collectives and lax.ppermute only.
A program may use at most 128 MiB of HBM per device.

v0:
```python
import jax
import jax.numpy as jnp
import numpy as np
from jax import lax
from jax.sharding import PartitionSpec as P

RATIO = 4
REACH = 4
CREACH = 2
PTILES = 3
FSPAN = 1
PFRAME = 5
QHALF = 3
BAND = 11


def extended(shard, sides, width):
    for axis, dim in sides:
        size, length = (lax.axis_size(axis), shard.shape[dim])
        up = [(i, (i + 1) % size) for i in range(size - 1)]
        down = [(j, i) for i, j in up]
        last = lax.slice_in_dim(shard, length - width, length, axis=dim)
        first = lax.slice_in_dim(shard, 0, width, axis=dim)
        before = lax.ppermute(last, axis, up)
        after = lax.ppermute(first, axis, down)
        shard = jnp.concatenate([before, shard, after], axis=dim)
    return shard


def from_behind(shard, axis, by):
    length = lax.axis_size(axis)
    pairs = [(i, i + by) for i in range(length) if 0 <= i + by < length]
    return lax.ppermute(shard, axis, pairs)


def make_slots(columns, counts, panel_ids):
    centre = panel_ids // RATIO
    slot_index = columns - centre[:, None] + CREACH
    live = jnp.arange(PTILES, dtype=jnp.int32)[None, :] < counts[:, None]
    return jnp.where(live, slot_index, -1)


def expand_frames(tiles, slots):
    select = (slots[:, :, None] == jnp.arange(PFRAME, dtype=jnp.int32)[None, None, :]).astype(
        jnp.bfloat16
    )
    frame = jnp.einsum("nqs,nqpc->npsc", select, tiles, preferred_element_type=jnp.float32)
    return frame.reshape(tiles.shape[0], tiles.shape[2], PFRAME * tiles.shape[3]).astype(
        jnp.bfloat16
    )


def on_device(
    operator_tiles,
    operator_columns,
    operator_counts,
    prolong_tiles,
    prolong_columns,
    prolong_counts,
):
    local_count = operator_columns.shape[0]
    coarse_local = local_count // RATIO
    panel_rows = operator_tiles.shape[2]
    coarse_width = prolong_tiles.shape[3]
    tile_slots = operator_tiles.shape[1]
    device = lax.axis_index(("row", "grp"))
    first_panel = device * local_count
    panel_ids = first_panel + jnp.arange(local_count, dtype=jnp.int32)
    slot_table = make_slots(prolong_columns, prolong_counts, panel_ids)
    own_frames = expand_frames(prolong_tiles, slot_table)
    frames = extended(own_frames, ((("row", "grp"), 0),), REACH)
    offset_count = 2 * REACH + 1
    width_f = PFRAME * coarse_width
    width_q = (2 * QHALF + 1) * coarse_width
    offset_values = jnp.arange(offset_count, dtype=jnp.int32) - REACH
    slot_ids = jnp.arange(tile_slots, dtype=jnp.int32)
    live_slots = slot_ids[None, :] < operator_counts[:, None]
    distance = operator_columns - panel_ids[:, None]
    selector = (
        (distance[:, :, None] == offset_values[None, None, :]) & live_slots[:, :, None]
    ).astype(jnp.bfloat16)
    by_offset = jnp.einsum(
        "fkd,fkpr->fdpr", selector, operator_tiles, preferred_element_type=jnp.float32
    )
    by_offset = by_offset.astype(jnp.bfloat16).reshape(
        coarse_local, RATIO, offset_count, panel_rows, panel_rows
    )
    phase_rows = []
    for phase_index in range(RATIO):
        lookup_table = np.array(
            [
                [
                    phase_index + offset_slot + coarse_slot * RATIO
                    for offset_slot in range(offset_count)
                ]
                for coarse_slot in range(coarse_local)
            ],
            dtype=np.int32,
        )
        frame_window = frames[jnp.asarray(lookup_table)]
        phase_sum = jnp.zeros((coarse_local, panel_rows, width_q), jnp.float32)
        for block_index in range(2 * FSPAN + 1):
            chosen_offsets = [
                offset_slot
                for offset_slot in range(offset_count)
                if (phase_index + offset_slot - REACH) // RATIO + FSPAN == block_index
            ]
            lowest = chosen_offsets[0]
            highest = chosen_offsets[-1] + 1
            term = jnp.einsum(
                "cdpr,cdrw->cpw",
                by_offset[:, phase_index, lowest:highest],
                frame_window[:, lowest:highest],
                preferred_element_type=jnp.float32,
            )
            start = block_index * coarse_width
            phase_sum = phase_sum.at[:, :, start : start + width_f].add(term)
        phase_rows.append(phase_sum.astype(jnp.bfloat16))
    rounded = jnp.stack(phase_rows, axis=1)
    own_split = own_frames.reshape(coarse_local, RATIO, panel_rows, PFRAME, coarse_width)
    contribution = jnp.einsum(
        "cipsa,cipw->csaw", own_split, rounded, preferred_element_type=jnp.float32
    )
    accumulated = jnp.zeros(
        (coarse_local + 2 * CREACH, coarse_width, BAND * coarse_width), jnp.float32
    )
    for slot_s in range(PFRAME):
        start = (2 * CREACH - slot_s) * coarse_width
        accumulated = accumulated.at[
            slot_s : slot_s + coarse_local, :, start : start + width_q
        ].add(contribution[:, slot_s])
    from_next = from_behind(accumulated[:CREACH], ("row", "grp"), -1)
    from_prev = from_behind(accumulated[coarse_local + CREACH :], ("row", "grp"), 1)
    result = accumulated[CREACH : CREACH + coarse_local]
    result = result.at[coarse_local - CREACH :].add(from_next)
    result = result.at[:CREACH].add(from_prev)
    return result


def solution(mesh):
    placed = (
        P(("row", "grp"), None, None, None),
        P(("row", "grp"), None),
        P(("row", "grp")),
        P(("row", "grp"), None, None, None),
        P(("row", "grp"), None),
        P(("row", "grp")),
    )
    return jax.shard_map(
        on_device,
        mesh=mesh,
        in_specs=placed,
        out_specs=P(("row", "grp"), None, None),
        check_vma=False,
    )
```

profile of v0, /device:TPU:6, one launch (start us, length us, event | category | flops | bytes accessed | tf_op | source)
XLA Modules:
  0.0 216.9 jit_solution(11435971990382669917)
XLA Ops:
  1.4 2.0 convolution_convert_fusion.1
  3.5 3.1 %fusion.117 = (bf16[4,256,5,128]{3,2,1,0:T(8,128)(2,1)}, bf16[4,256,5,128]{3,2,1,0:T(8,128)(2,1)}) fusion(bf16[8,256,5,128]{3,2,1,0:T(8,128)(2,1)S(1)} %bitcast.178), kind=kLoop, calls=%fused_computation.124 | loop fusion | bytes 5242880 | tf_op jit(solution)/shard_map/slice | solution.py:22
  6.8 4.1 %copy.38 = bf16[4,256,5,128]{1,3,2,0:T(8,128)(2,1)} copy(bf16[4,256,5,128]{3,2,1,0:T(8,128)(2,1)} %get-tuple-element.263) | data formatting | bytes 2621440 | tf_op jit(solution)/shard_map/slice | solution.py:22
  10.9 1.9 collective-permute-start
  12.8 4.1 %copy.40 = bf16[4,256,5,128]{1,3,2,0:T(8,128)(2,1)} copy(bf16[4,256,5,128]{3,2,1,0:T(8,128)(2,1)} %get-tuple-element.264) | data formatting | bytes 2621440 | tf_op jit(solution)/shard_map/slice | solution.py:23
  16.9 8.4 %collective-permute-start.1 = (bf16[4,256,640]{1,2,0:T(8,128)(2,1)}, bf16[4,256,640]{1,2,0:T(8,128)(2,1)}, u32[]{:S(2)}, u32[]{:S(2)}) collective-permute-start(bf16[4,256,640]{1,2,0:T(8,128)(2,1)} %bitcast.10), channel_id=1, source_target_pairs={{1,0},{2,1},{3,2},{4,3},{5,4},{6,5},{7,6},{8,7},{9,8},{10,9},{11,1... | collective-permute-start | bytes 3932168 | tf_op jit(solution)/shard_map/ppermute | solution.py:25
  25.3 6.2 %copy.39 = bf16[8,256,5,128]{1,3,2,0:T(8,128)(2,1)} copy(bf16[8,256,5,128]{3,2,1,0:T(8,128)(2,1)} %bitcast.179) | data formatting | bytes 5242880 | tf_op jit(solution)/shard_map/convert_element_type | solution.py:48
  31.6 17.2 %convolution_convert_fusion = bf16[8,9,256,256]{3,1,2,0:T(8,128)(2,1)S(1)} fusion(bf16[8,8,256,256]{3,2,1,0:T(8,128)(2,1)} %param.52, s32[9]{0:T(128)S(1)} %iota_add_fusion, s32[8,8]{1,0:T(8,128)S(1)} %broadcast_subtract_fusion, pred[8,8]{1,0:T(8,128)(4,1)S(1)} %iota_compare_fusion.1), kind=kOutput, calls=%fused_computation.4 | convolution fusion | flops 80217216 | bytes 17826148 | tf_op jit(solution)/shard_map/fkd,fkpr->fdpr/dot_general | solution.py:82
  48.8 1.6 fusion.112
  50.4 1.9 fusion.115
  53.1 2.0 and_reduce_fusion
  55.1 1.8 fusion.114
  56.8 4.3 %fusion.113 = (bf16[2,1,4,256,256]{4,2,3,1,0:T(4,128)(2,1)}, bf16[2,1,4,256,256]{4,2,3,1,0:T(4,128)(2,1)}, bf16[2,1,4,256,256]{4,2,3,1,0:T(4,128)(2,1)}, bf16[2,...) fusion(bf16[2,4,9,256,256]{4,2,3,1,0:T(8,128)(2,1)S(1)} %bitcast.184), kind=kLoop, calls=%fused_computation.120 | loop fusion | bytes 12582912 | tf_op jit(solution)/shard_map/slice | solution.py:112
  61.2 4.1 %pad_maximum_fusion = bf16[16,256,640]{1,2,0:T(8,128)(2,1)} fusion(bf16[4,256,640]{1,2,0:T(8,128)(2,1)} %collective-permute-done.1, bf16[8,256,640]{1,2,0:T(8,128)(2,1)S(1)} %bitcast.189, bf16[4,256,640]{1,2,0:T(8,128)(2,1)S(1)} %collective-permute-done), kind=kLoop, calls=%fused_computation.6 | loop fusion | flops 5242880 | bytes 10485760 | tf_op jit(solution)/shard_map/concatenate | solution.py:26
  65.2 7.0 %gather_fusion = bf16[18,256,640]{1,2,0:T(8,128)(2,1)} fusion(bf16[16,256,640]{1,2,0:T(8,128)(2,1)} %pad_maximum_fusion, s32[1024]{0:T(1024)S(1)} %pad_clamp_fusion.3), kind=kCustom, calls=%fused_computation | custom fusion | bytes 11796552 | tf_op jit(solution)/shard_map/gather | solution.py:100
  72.3 8.9 %copy.41 = bf16[18,256,640]{2,1,0:T(8,128)(2,1)} copy(bf16[18,256,640]{1,2,0:T(8,128)(2,1)} %gather_fusion) | data formatting | bytes 11796480 | tf_op jit(solution)/shard_map/gather | solution.py:100
  81.2 3.2 %fusion.27 = f32[2,256,640]{2,1,0:T(8,128)S(1)} fusion(bf16[2,9,256,640]{3,2,1,0:T(8,128)(2,1)} %bitcast.193, bf16[2,1,4,256,256]{4,2,3,1,0:T(4,128)(2,1)} %get-tuple-element.254), kind=kOutput, calls=%fused_computation.32 | convolution fusion | flops 671088640 | bytes 4980736 | tf_op jit(solution)/shard_map/cdpr,cdrw->cpw/dot_general | solution.py:110
  85.7 1.1 fusion.85
  87.2 1.0 convert_bitcast_fusion.3
  88.3 7.0 %gather_fusion.3 = bf16[18,256,640]{1,2,0:T(8,128)(2,1)} fusion(bf16[16,256,640]{1,2,0:T(8,128)(2,1)} %pad_maximum_fusion, s32[1024]{0:T(1024)S(1)} %pad_clamp_fusion), kind=kCustom, calls=%fused_computation.3 | custom fusion | bytes 11796552 | tf_op jit(solution)/shard_map/gather | solution.py:100
  95.3 8.9 %copy.53 = bf16[18,256,640]{2,1,0:T(8,128)(2,1)} copy(bf16[18,256,640]{1,2,0:T(8,128)(2,1)} %gather_fusion.3) | data formatting | bytes 11796480 | tf_op jit(solution)/shard_map/gather | solution.py:100
  104.2 1.7 fusion.102
  106.1 2.9 %fusion.67 = f32[2,256,896]{2,1,0:T(8,128)S(1)} fusion(f32[2,256,896]{2,1,0:T(8,128)S(1)} %scatter-add.71, bf16[2,9,256,640]{3,2,1,0:T(8,128)(2,1)} %bitcast.196, bf16[2,1,4,256,256]{4,2,3,1,0:T(4,128)(2,1)S(1)} %copy-done.13), kind=kOutput, calls=%fused_computation.49 | convolution fusion | flops 671416320 | bytes 6291456 | tf_op jit(solution)/shard_map/cdpr,cdrw->cpw/dot_general | solution.py:110
  109.0 2.8 %fusion.61 = f32[2,256,896]{2,1,0:T(8,128)S(1)} fusion(f32[2,256,896]{2,1,0:T(8,128)S(1)} %fusion.67, bf16[2,9,256,640]{3,2,1,0:T(8,128)(2,1)} %bitcast.197, bf16[2,1,4,256,256]{4,2,3,1,0:T(4,128)(2,1)S(1)} %copy-done.12), kind=kOutput, calls=%fused_computation.47 | convolution fusion | flops 671416320 | bytes 6291456 | tf_op jit(solution)/shard_map/cdpr,cdrw->cpw/dot_general | solution.py:110
  112.8 7.0 %gather_fusion.1 = bf16[18,256,640]{1,2,0:T(8,128)(2,1)} fusion(bf16[16,256,640]{1,2,0:T(8,128)(2,1)} %pad_maximum_fusion, s32[1024]{0:T(1024)S(1)} %pad_clamp_fusion.2), kind=kCustom, calls=%fused_computation.1 | custom fusion | bytes 11796552 | tf_op jit(solution)/shard_map/gather | solution.py:100
  119.8 8.9 %copy.45 = bf16[18,256,640]{2,1,0:T(8,128)(2,1)} copy(bf16[18,256,640]{1,2,0:T(8,128)(2,1)} %gather_fusion.1) | data formatting | bytes 11796480 | tf_op jit(solution)/shard_map/gather | solution.py:100
  128.7 2.8 %fusion.46 = f32[2,256,640]{2,1,0:T(8,128)S(1)} fusion(bf16[2,9,256,640]{3,2,1,0:T(8,128)(2,1)} %bitcast.190, bf16[2,1,3,256,256]{4,2,3,1,0:T(4,128)(2,1)} %get-tuple-element.259), kind=kOutput, calls=%fused_computation.42 | convolution fusion | flops 503316480 | bytes 4325376 | tf_op jit(solution)/shard_map/cdpr,cdrw->cpw/dot_general | solution.py:110
  132.9 1.1 fusion.79
  134.6 1.0 convert_bitcast_fusion.2
  135.7 7.0 %gather_fusion.2 = bf16[18,256,640]{1,2,0:T(8,128)(2,1)} fusion(bf16[16,256,640]{1,2,0:T(8,128)(2,1)} %pad_maximum_fusion, s32[1024]{0:T(1024)S(1)} %pad_clamp_fusion.1), kind=kCustom, calls=%fused_computation.2 | custom fusion | bytes 11796552 | tf_op jit(solution)/shard_map/gather | solution.py:100
  142.7 8.9 %copy.49 = bf16[18,256,640]{2,1,0:T(8,128)(2,1)} copy(bf16[18,256,640]{1,2,0:T(8,128)(2,1)} %gather_fusion.2) | data formatting | bytes 11796480 | tf_op jit(solution)/shard_map/gather | solution.py:100
  151.7 2.1 convolution_bitcast_fusion
  154.7 2.3 %fusion.73 = f32[2,256,896]{2,1,0:T(8,128)S(1)} fusion(f32[2,256,896]{2,1,0:T(8,128)S(1)} %scatter-add.66, bf16[2,9,256,640]{3,2,1,0:T(8,128)(2,1)S(1)} %bitcast.187, bf16[2,1,4,256,256]{4,2,3,1,0:T(4,128)(2,1)} %get-tuple-element.252), kind=kOutput, calls=%fused_computation.51 | convolution fusion | flops 671416320 | bytes 6291456 | tf_op jit(solution)/shard_map/cdpr,cdrw->cpw/dot_general | solution.py:110
  158.0 1.2 copy-done.3
  160.2 3.2 %fusion.16 = f32[2,5,128,896]{3,2,1,0:T(8,128)S(1)} fusion(bf16[2,4,256,5,128]{4,3,2,1,0:T(8,128)(2,1)S(1)} %bitcast.180, bf16[2,1,256,896]{3,2,0,1:T(8,128)(2,1)S(1)} %copy-done.16, bf16[2,1,256,896]{3,2,0,1:T(8,128)(2,1)S(1)} %convert_bitcast_fusion.1, bf16[2,1,256,896]{3,2,0,1:T(8,128)(2,1)S(1)} %copy-done.17, bf16[2,1,256,896]{3,2,0,1:T(8,128)(2,1)S(1)} %copy-done.15), kind=kOutput, calls=%fused_computation.24 | convolution fusion | flops 2354315264 | bytes 10878976 | tf_op jit(solution)/shard_map/cipsa,cipw->csaw/dot_general | solution.py:121
  163.4 2.1 copy-done.8
  166.2 2.4 %broadcast_in_dim.14 = f32[6,128,1408]{2,1,0:T(8,128)} broadcast(f32[]{:T(128)} %constant.502.clone.1), dimensions={} | broadcast | bytes 4325380 | tf_op jit(solution)/shard_map/broadcast_in_dim | solution.py:124
  168.6 6.2 %scatter-add.76 = f32[6,128,1408]{2,1,0:T(8,128)} dynamic-update-slice(f32[6,128,1408]{2,1,0:T(8,128)} %broadcast_in_dim.14, f32[2,128,896]{2,1,0:T(8,128)S(1)} %fusion.101, s32[]{:T(128)} %bitcast.57, s32[]{:T(128)} %constant.503.clone.1, s32[]{:T(128)} %bitcast.58) | dynamic-update-slice | bytes 1835012 | tf_op jit(solution)/shard_map/scatter-add | solution.py:131
  174.8 2.5 %fusion.99 = f32[6,128,1408]{2,1,0:T(8,128)} fusion(f32[6,128,1408]{2,1,0:T(8,128)} %scatter-add.76, f32[2,5,128,896]{3,2,1,0:T(8,128)} %copy-done.8), kind=kLoop, calls=%fused_computation.77 | loop fusion | flops 229376 | bytes 2752512 | tf_op jit(solution)/shard_map/scatter-add | solution.py:131
  177.3 2.5 %fusion.97 = f32[6,128,1408]{2,1,0:T(8,128)} fusion(f32[6,128,1408]{2,1,0:T(8,128)} %fusion.99, f32[2,5,128,896]{3,2,1,0:T(8,128)} %copy-done.8), kind=kLoop, calls=%fused_computation.74 | loop fusion | flops 229376 | bytes 2752512 | tf_op jit(solution)/shard_map/scatter-add | solution.py:131
  179.8 2.5 %fusion.95 = f32[6,128,1408]{2,1,0:T(8,128)} fusion(f32[6,128,1408]{2,1,0:T(8,128)} %fusion.97, f32[2,5,128,896]{3,2,1,0:T(8,128)} %copy-done.8), kind=kLoop, calls=%fused_computation.71 | loop fusion | flops 229376 | bytes 2752512 | tf_op jit(solution)/shard_map/scatter-add | solution.py:131
  182.3 2.5 %fusion.93 = f32[6,128,1408]{2,1,0:T(8,128)} fusion(f32[6,128,1408]{2,1,0:T(8,128)} %fusion.95, f32[2,5,128,896]{3,2,1,0:T(8,128)} %copy-done.8), kind=kLoop, calls=%fused_computation.68 | loop fusion | flops 229376 | bytes 2752512 | tf_op jit(solution)/shard_map/scatter-add | solution.py:131
  184.8 2.0 fusion.116
  186.8 2.6 %collective-permute-start.2 = (f32[2,128,1408]{2,1,0:T(8,128)S(1)}, f32[2,128,1408]{2,1,0:T(8,128)S(1)}, u32[]{:S(2)}, u32[]{:S(2)}) collective-permute-start(f32[2,128,1408]{2,1,0:T(8,128)S(1)} %get-tuple-element.261), channel_id=1, source_target_pairs={{1,0},{2,1},{3,2},{4,3},{5,4},{6,5},{7,6},{8,7},{9,8},{10,9},{11,1... | collective-permute-start | bytes 4325384 | tf_op jit(solution)/shard_map/ppermute | solution.py:33
  189.4 2.1 collective-permute-start.3
  191.5 14.4 %collective-permute-done.2 = f32[2,128,1408]{2,1,0:T(8,128)S(1)} collective-permute-done((f32[2,128,1408]{2,1,0:T(8,128)S(1)}, f32[2,128,1408]{2,1,0:T(8,128)S(1)}, u32[]{:S(2)}, u32[]{:S(2)}) %collective-permute-start.2) | collective-permute-done | bytes 1441824 | tf_op jit(solution)/shard_map/ppermute | solution.py:33
  205.9 8.2 %collective-permute-done.3 = f32[2,128,1408]{2,1,0:T(8,128)S(1)} collective-permute-done((f32[2,128,1408]{2,1,0:T(8,128)S(1)}, f32[2,128,1408]{2,1,0:T(8,128)S(1)}, u32[]{:S(2)}, u32[]{:S(2)}) %collective-permute-start.3) | collective-permute-done | bytes 1441824 | tf_op jit(solution)/shard_map/ppermute | solution.py:33
  214.1 2.8 %fusion.26 = f32[2,128,1408]{2,1,0:T(8,128)} fusion(f32[2,128,1408]{2,1,0:T(8,128)S(1)} %collective-permute-done.3, f32[2,128,1408]{2,1,0:T(8,128)S(1)} %collective-permute-done.2, f32[6,128,1408]{2,1,0:T(8,128)} %fusion.93), kind=kLoop, calls=%fused_computation.31 | loop fusion | flops 720896 | bytes 5767168 | tf_op jit(solution)/shard_map/add | solution.py:136
  (72 shorter events, 11.1 us)
Async XLA Ops:
  0.0 1.4 copy-start
  3.5 3.3 %copy-start.2 = (bf16[8,5,256,128]{3,1,2,0:T(8,128)(2,1)}, bf16[8,5,256,128]{3,1,2,0:T(8,128)(2,1)S(1)}, u32[]{:S(2)}) copy-start(bf16[8,5,256,128]{3,1,2,0:T(8,128)(2,1)S(1)} %convolution_convert_fusion.1) | copy-start | bytes 7864324
  10.9 50.3 %collective-permute-start = (bf16[4,256,640]{1,2,0:T(8,128)(2,1)}, bf16[4,256,640]{1,2,0:T(8,128)(2,1)S(1)}, u32[]{:S(2)}, u32[]{:S(2)}) collective-permute-start(bf16[4,256,640]{1,2,0:T(8,128)(2,1)} %bitcast.8), channel_id=1, source_target_pairs={{0,1},{1,2},{2,3},{3,4},{4,5},{5,6},{6,7},{7,8},{8,9},{9,10},{10,1... | collective-permute-start | bytes 3932168 | tf_op jit(solution)/shard_map/ppermute | solution.py:24
  16.9 14.6 %copy-start.24 = (s32[8]{0:T(128)S(1)}, s32[8]{0:T(128)}, u32[]{:S(2)}) copy-start(s32[8]{0:T(128)} %param.54) | copy-start | bytes 100
  16.9 14.7 %copy-start.18 = (s32[8,8]{1,0:T(8,128)S(1)}, s32[8,8]{1,0:T(8,128)}, u32[]{:S(2)}) copy-start(s32[8,8]{1,0:T(8,128)} %param.53) | copy-start | bytes 772
  16.9 44.3 %collective-permute-start.1 = (bf16[4,256,640]{1,2,0:T(8,128)(2,1)}, bf16[4,256,640]{1,2,0:T(8,128)(2,1)}, u32[]{:S(2)}, u32[]{:S(2)}) collective-permute-start(bf16[4,256,640]{1,2,0:T(8,128)(2,1)} %bitcast.10), channel_id=1, source_target_pairs={{1,0},{2,1},{3,2},{4,3},{5,4},{6,5},{7,6},{8,7},{9,8},{10,9},{11,1... | collective-permute-start | bytes 3932168 | tf_op jit(solution)/shard_map/ppermute | solution.py:25
  50.4 2.0 copy-start.23
  50.4 2.0 copy-start.22
  50.4 2.0 copy-start.21
  50.4 2.7 %copy-start.20 = (s32[3]{0:T(128)S(1)}, s32[3]{0:T(128)}, u32[]{:S(2)}) copy-start(s32[3]{0:T(128)} %constant.506.clone.1) | copy-start | bytes 40
  50.4 4.6 %copy-start.19 = (s32[18]{0:T(128)S(1)}, s32[18]{0:T(128)}, u32[]{:S(2)}) copy-start(s32[18]{0:T(128)} %constant.558) | copy-start | bytes 220
  56.8 4.4 %copy-start.5 = (bf16[8,256,5,128]{1,3,2,0:T(8,128)(2,1)S(1)}, bf16[8,256,5,128]{1,3,2,0:T(8,128)(2,1)}, u32[]{:S(2)}) copy-start(bf16[8,256,5,128]{1,3,2,0:T(8,128)(2,1)} %copy.39) | copy-start | bytes 7864324
  81.2 3.8 %copy-start.7 = (bf16[18,256,640]{2,1,0:T(8,128)(2,1)S(1)}, bf16[18,256,640]{2,1,0:T(8,128)(2,1)}, u32[]{:S(2)}) copy-start(bf16[18,256,640]{2,1,0:T(8,128)(2,1)} %copy.41) | copy-start | bytes 17694724
  84.4 1.4 copy-start.14
  85.7 1.1 copy-start.10
  104.2 1.9 copy-start.13
  106.1 2.9 %copy-start.12 = (bf16[2,1,4,256,256]{4,2,3,1,0:T(4,128)(2,1)S(1)}, bf16[2,1,4,256,256]{4,2,3,1,0:T(4,128)(2,1)}, u32[]{:S(2)}) copy-start(bf16[2,1,4,256,256]{4,2,3,1,0:T(4,128)(2,1)} %get-tuple-element.255) | copy-start | bytes 3145732
  128.7 3.6 %copy-start.6 = (bf16[18,256,640]{2,1,0:T(8,128)(2,1)S(1)}, bf16[18,256,640]{2,1,0:T(8,128)(2,1)}, u32[]{:S(2)}) copy-start(bf16[18,256,640]{2,1,0:T(8,128)(2,1)} %copy.45) | copy-start | bytes 17694724
  131.5 1.4 copy-start.11
  142.7 8.9 %copy-start.9 = (bf16[2,1,2,256,256]{4,2,3,1,0:T(2,128)(2,1)S(1)}, bf16[2,1,2,256,256]{4,2,3,1,0:T(2,128)(2,1)}, u32[]{:S(2)}) copy-start(bf16[2,1,2,256,256]{4,2,3,1,0:T(2,128)(2,1)} %get-tuple-element.258) | copy-start | bytes 1572868
  151.7 3.1 %copy-start.4 = (bf16[18,256,640]{2,1,0:T(8,128)(2,1)S(1)}, bf16[18,256,640]{2,1,0:T(8,128)(2,1)}, u32[]{:S(2)}) copy-start(bf16[18,256,640]{2,1,0:T(8,128)(2,1)} %copy.49) | copy-start | bytes 17694724
  157.0 2.2 %copy-start.3 = (bf16[8,5,256,128]{3,1,2,0:T(8,128)(2,1)S(1)}, bf16[8,5,256,128]{3,1,2,0:T(8,128)(2,1)}, u32[]{:S(2)}) copy-start(bf16[8,5,256,128]{3,1,2,0:T(8,128)(2,1)} %copy-done.2) | copy-start | bytes 7864324
  157.9 1.8 copy-start.15
  157.9 2.1 copy-start.16
  157.9 2.3 %copy-start.17 = (bf16[2,1,256,896]{3,2,0,1:T(8,128)(2,1)S(1)}, bf16[2,1,256,896]{3,2,0,1:T(8,128)(2,1)}, u32[]{:S(2)}) copy-start(bf16[2,1,256,896]{3,2,0,1:T(8,128)(2,1)} %convert_bitcast_fusion.2) | copy-start | bytes 2752516
  163.4 2.1 copy-start.8
  186.8 19.1 %collective-permute-start.2 = (f32[2,128,1408]{2,1,0:T(8,128)S(1)}, f32[2,128,1408]{2,1,0:T(8,128)S(1)}, u32[]{:S(2)}, u32[]{:S(2)}) collective-permute-start(f32[2,128,1408]{2,1,0:T(8,128)S(1)} %get-tuple-element.261), channel_id=1, source_target_pairs={{1,0},{2,1},{3,2},{4,3},{5,4},{6,5},{7,6},{8,7},{9,8},{10,9},{11,1... | collective-permute-start | bytes 4325384 | tf_op jit(solution)/shard_map/ppermute | solution.py:33
  189.4 27.5 %copy-start.1 = (bf16[8,3,256,128]{3,2,1,0:T(8,128)(2,1)S(1)}, bf16[8,3,256,128]{3,2,1,0:T(8,128)(2,1)}, u32[]{:S(2)}) copy-start(bf16[8,3,256,128]{3,2,1,0:T(8,128)(2,1)} %param.55) | copy-start | bytes 4718596
  189.4 24.7 %collective-permute-start.3 = (f32[2,128,1408]{2,1,0:T(8,128)S(1)}, f32[2,128,1408]{2,1,0:T(8,128)S(1)}, u32[]{:S(2)}, u32[]{:S(2)}) collective-permute-start(f32[2,128,1408]{2,1,0:T(8,128)S(1)} %get-tuple-element.262), channel_id=1, source_target_pairs={{0,1},{1,2},{2,3},{3,4},{4,5},{5,6},{6,7},{7,8},{8,9},{9,10},{10,1... | collective-permute-start | bytes 4325384 | tf_op jit(solution)/shard_map/ppermute | solution.py:33
where the time goes:
time: 219 us; the launch traced here: 217 us
  local copies, waits for them, and re-layouts  111 us (51%)
  matrix products  44.2 us (20%)
  other arithmetic  23.7 us (11%)
  waiting for transfers between devices  22.6 us (10%)
  starting transfers between devices  14.9 us (7%)
    gather x8, local copies, waits for them, and re-layouts, on_device(): frame_window = frames[jnp.asarray(lookup_table)]  63.7 us
    ppermute x2, waiting for transfers between devices, from_behind(): return lax.ppermute(shard, axis, pairs)  22.6 us
    dot_general x12, matrix products, on_device(): jnp.einsum('cdpr,cdrw->cpw', by_offset[:, phase_index, lowest:highest], f...  21.8 us
    dot_general x1, matrix products, on_device(): jnp.einsum('fkd,fkpr->fdpr', selector, operator_tiles, preferred_element_...  17.2 us
    scatter-add x4, other arithmetic, on_device(): accumulated = accumulated.at[slot_s:slot_s + coarse_local, :, start:start...  10 us
    slice x4, local copies, waits for them, and re-layouts, on_device(): by_offset[:, phase_index, lowest:highest]  9.6 us
    unnamed x50, local copies, waits for them, and re-layouts  8.48 us
    ppermute x1, starting transfers between devices, extended(): after = lax.ppermute(first, axis, down)  8.4 us
  transfers between devices with their start and end apart: 4, of which 2 were waited for; matrix products, arithmetic and copies ran while one was open for 18% of the time, Pallas kernels for 0%

commit v1 on v0

v1 whole, which is shorter than its diff:
```python
import jax
import jax.numpy as jnp
from jax import lax
from jax.experimental import pallas as pl
from jax.experimental.pallas import tpu as pltpu
from jax.sharding import PartitionSpec as P

AXES = ("row", "grp")
PANEL = 256
CP = 128
HALF = 4
SLOTS = 3
BAND = 11
DEAD = 7
PAY_ROWS = HALF * SLOTS * PANEL
META_ROWS = 16
VMEM_LIMIT = 48 * 1024 * 1024


def device_id():
    grp = lax.axis_index("grp")
    return lax.axis_index("row") * lax.axis_size("grp") + grp, lax.rem(grp, 2)


def slot_of(columns, counts, device, panel, slot):
    s = columns[panel, slot] - (2 * device + lax.div(panel, HALF)) + 2
    return jnp.where(slot < counts[panel], s, DEAD)


def tile_at(ref, index):
    return ref[pl.ds(pl.multiple_of(index * PANEL, PANEL), PANEL), :]


def three(ref, panel):
    return jnp.concatenate([tile_at(ref, panel * SLOTS + t) for t in range(SLOTS)], axis=1)


def dot(a, b):
    return jnp.dot(a, b, preferred_element_type=jnp.float32)


def dot_t(a, b):
    return lax.dot_general(a, b, (((0,), (0,)), ((), ())), preferred_element_type=jnp.float32)


def pack_kernel(columns, counts, tiles, on_ref, off_ref, meta, sems):
    device, parity = device_id()
    copies = []
    for at, (ref, half) in enumerate(((off_ref, parity), (on_ref, 1 - parity))):
        copies.append(
            pltpu.make_async_copy(
                tiles.at[pl.ds(pl.multiple_of(half * PAY_ROWS, PAY_ROWS), PAY_ROWS)],
                ref.at[pl.ds(0, PAY_ROWS)],
                sems.at[2 * at],
            )
        )
        copies[-1].start()
    lane = lax.broadcasted_iota(jnp.int32, (META_ROWS, CP), 1)
    for at, (ref, half) in enumerate(((off_ref, parity), (on_ref, 1 - parity))):
        values = jnp.zeros((META_ROWS, CP), jnp.int32)
        for p in range(HALF):
            for t in range(SLOTS):
                s = slot_of(columns, counts, device, half * HALF + p, t)
                values = jnp.where(lane == p * SLOTS + t, s, values)
        meta[at] = values.astype(jnp.float32).astype(jnp.bfloat16)
        copies.append(
            pltpu.make_async_copy(meta.at[at], ref.at[pl.ds(PAY_ROWS, META_ROWS)], sems.at[2 * at + 1])
        )
        copies[-1].start()
    for copy in copies:
        copy.wait()


def border_kernel(ocols, ocnt, pcols, pcnt, oper, tiles, out, abuf, px, acc, asem, psem):
    device, parity = device_id()

    def case(il, k):
        i = parity * HALF + il
        j = ocols[i, k] - 8 * device
        jo = jnp.where(parity == 1, j - 8, j + HALF)
        hit = (k < ocnt[i]) & (jo >= 0) & (jo < HALF)
        return i, jnp.clip(jo, 0, HALF - 1), hit

    p_copy = pltpu.make_async_copy(
        tiles.at[pl.ds(pl.multiple_of(parity * PAY_ROWS, PAY_ROWS), PAY_ROWS)], px, psem.at[0]
    )
    p_copy.start()

    def a_copy(il, k, i):
        return pltpu.make_async_copy(oper.at[i, k], abuf.at[il * 8 + k], asem.at[il * 8 + k])

    for il in range(HALF):
        for k in range(1, 8):
            i, _, hit = case(il, k)

            @pl.when(hit)
            def _():
                a_copy(il, k, i).start()

    acc[...] = jnp.zeros_like(acc)
    p_copy.wait()
    for il in range(HALF):
        i0 = parity * HALF + il
        rows = []
        for t in range(1, SLOTS):
            s = slot_of(pcols, pcnt, device, i0, t)
            r = parity + s - 2
            near = (parity == 1) & (r == 2) | (parity == 0) & (r == -1)
            far = (parity == 1) & (r == 3) | (parity == 0) & (r == -2)
            live = s < DEAD
            rows.append(jnp.where(live & near, 0, jnp.where(live & far, 1, 2)))
        for k in range(1, 8):
            i, jo, hit = case(il, k)

            @pl.when(hit)
            def _():
                a_copy(il, k, i).wait()
                lhs = jnp.concatenate([tile_at(px, il * SLOTS + 1), tile_at(px, il * SLOTS + 2)], axis=1)
                res = dot_t(lhs, abuf[il * 8 + k])
                for t in range(2):
                    acc[rows[t] * HALF + jo] += res[t * CP : (t + 1) * CP]

    for jo in range(HALF):
        for near in range(2):
            out[(jo * 2 + near) * CP : (jo * 2 + near + 1) * CP, :] = acc[near * HALF + jo].astype(jnp.bfloat16)


def local_kernel(
    ocols, ocnt, pcols, pcnt, oper, tiles, pay, roff, ron, own, abuf, px, prod, acc, meta_v, meta_s, slots, asem, psem
):
    device, parity = device_id()
    on = 1 - parity
    copies = [
        pltpu.make_async_copy(tiles, px.at[pl.ds(0, 2 * PAY_ROWS)], psem.at[0]),
        pltpu.make_async_copy(pay.at[pl.ds(0, PAY_ROWS)], px.at[pl.ds(2 * PAY_ROWS, PAY_ROWS)], psem.at[1]),
        pltpu.make_async_copy(pay.at[pl.ds(PAY_ROWS, META_ROWS)], meta_v.at[0], psem.at[2]),
    ]
    for copy in copies[::-1]:
        copy.start()

    def a_copy(i):
        return pltpu.make_async_copy(oper.at[i], abuf.at[i], asem.at[i])

    for i in range(8):
        a_copy(i).start()
    for i in range(8):
        for t in range(SLOTS):
            slots[i * SLOTS + t] = slot_of(pcols, pcnt, device, i, t)

    @pl.loop(0, 56)
    def _(n):
        acc[n] = jnp.zeros((CP, CP), jnp.float32)

    copies[2].wait()
    meta_i = meta_v[0].astype(jnp.float32).astype(jnp.int32)
    read_meta(meta_i, meta_s, slots, 8 * SLOTS)
    copies[0].wait()
    copies[1].wait()

    @pl.loop(0, 8)
    def _(i):
        m = lax.div(i, HALF)
        a_copy(i).wait()
        prod[...] = jnp.zeros_like(prod)

        def term(k):
            j = ocols[i, k] - 8 * device
            mine = (j >= 0) & (j < 8)
            jn = jnp.where(parity == 1, j + HALF, j - 8)
            theirs = (jn >= 0) & (jn < HALF)
            x = jnp.where(mine, j, jnp.where(theirs, 8 + jn, 0))
            live = (k < ocnt[i]) & (mine | theirs)
            base = lax.div(j + 8, HALF) - 2 - m + 1
            res = dot(abuf[i, k], three(px, x))
            for t in range(SLOTS):
                s = slots[x * SLOTS + t]
                q = jnp.where(live & (s < DEAD), base + s, 7)
                prod[q] += res[:, t * CP : (t + 1) * CP]

        for pair in range(4):
            if pair == 0:
                term(0)
                term(1)
            else:

                @pl.when(ocnt[i] > 2 * pair)
                def _(pair=pair):
                    term(2 * pair)
                    term(2 * pair + 1)

        rounded = jnp.concatenate([prod[q].astype(jnp.bfloat16) for q in range(7)], axis=1)
        for t in range(SLOTS):
            s = slots[i * SLOTS + t]
            row = jnp.where(s < DEAD, m + s, 6)
            res = dot_t(tile_at(px, i * SLOTS + t), rounded)
            for q in range(7):
                acc[row * 8 + m + q] += res[:, q * CP : (q + 1) * CP]

    near_off = jnp.where(parity == 1, 4, 1)
    far_off = jnp.where(parity == 1, 5, 0)
    for p in range(7):
        roff[p] = acc[near_off * 8 + p + on].astype(jnp.bfloat16)
    for p in range(6):
        roff[7 + p] = acc[far_off * 8 + p + 1].astype(jnp.bfloat16)
    near_on = jnp.where(parity == 1, 1, 4)
    far_on = jnp.where(parity == 1, 0, 5)
    for p in range(8):
        ron[p] = acc[near_on * 8 + p]
    for p in range(7):
        ron[8 + p] = acc[far_on * 8 + p + on]
    for r in range(2):
        for b in range(BAND):
            cb = b - 2 + r
            if 0 <= cb < 8:
                own[r * BAND + b] = acc[(r + 2) * 8 + cb]
            else:
                own[r * BAND + b] = jnp.zeros((CP, CP), jnp.float32)


def read_meta(values, meta_s, slots, at):
    vec, smem, sem = meta_s
    vec[...] = values[:8]
    copy = pltpu.make_async_copy(vec, smem, sem.at[0])
    copy.start()
    copy.wait()
    for l in range(HALF * SLOTS):
        slots[at + l] = smem[0, l]


def remote_kernel(
    ocols, ocnt, pcols, pcnt, oper, tiles, pay, bpay, own1, ron1, own, ron,
    abuf, px, prod, acc, meta_v, meta_s, slots, asem, psem,
):
    device, parity = device_id()
    copies = [
        pltpu.make_async_copy(
            tiles.at[pl.ds(pl.multiple_of(parity * PAY_ROWS, PAY_ROWS), PAY_ROWS)],
            px.at[pl.ds(0, PAY_ROWS)],
            psem.at[0],
        ),
        pltpu.make_async_copy(pay.at[pl.ds(0, PAY_ROWS)], px.at[pl.ds(PAY_ROWS, PAY_ROWS)], psem.at[1]),
        pltpu.make_async_copy(pay.at[pl.ds(PAY_ROWS, META_ROWS)], meta_v.at[0], psem.at[2]),
    ]
    for copy in copies[::-1]:
        copy.start()

    def case(il, k):
        i = parity * HALF + il
        j = ocols[i, k] - 8 * device
        jo = jnp.where(parity == 1, j - 8, j + HALF)
        hit = (k < ocnt[i]) & (jo >= 0) & (jo < HALF)
        return i, jnp.clip(jo, 0, HALF - 1), hit

    def a_copy(il, k, i):
        return pltpu.make_async_copy(oper.at[i, k], abuf.at[il * 8 + k], asem.at[il * 8 + k])

    for il in range(HALF):
        for k in range(1, 8):
            i, _, hit = case(il, k)

            @pl.when(hit)
            def _():
                a_copy(il, k, i).start()

    for il in range(HALF):
        for t in range(SLOTS):
            slots[il * SLOTS + t] = slot_of(pcols, pcnt, device, parity * HALF + il, t)

    for n in range(22):
        acc[n] = own1[n]
    for n in range(22, 32):
        acc[n] = jnp.zeros((CP, CP), jnp.float32)
    for p in range(8):
        acc[(1 - parity) * BAND + p + 3 * (1 - parity)] += ron1[p]
    for p in range(7):
        acc[parity * BAND + p + 4 * (1 - parity)] += ron1[8 + p]

    copies[2].wait()
    meta_i = meta_v[0].astype(jnp.float32).astype(jnp.int32)
    read_meta(meta_i, meta_s, slots, HALF * SLOTS)
    copies[0].wait()
    copies[1].wait()

    for il in range(HALF):
        res = dot(bpay[il * 2 * CP : (il + 1) * 2 * CP, :], three(px, il))
        for near in range(2):
            r = parity if near == 0 else 1 - parity
            for t in range(SLOTS):
                s = slots[il * SLOTS + t]
                at = jnp.where(s < DEAD, r * BAND + parity + s + 3 - r, 27)
                acc[at] += res[near * CP : (near + 1) * CP, t * CP : (t + 1) * CP]

    on_row = jnp.where(parity == 1, -1, 2)
    shift = jnp.where(parity == 1, 5, 2)
    for il in range(HALF):
        prod[...] = jnp.zeros_like(prod)
        for k in range(1, 8):
            i, jo, hit = case(il, k)

            @pl.when(hit)
            def _():
                a_copy(il, k, i).wait()
                res = dot(abuf[il * 8 + k], three(px, HALF + jo))
                for t in range(SLOTS):
                    s = slots[(HALF + jo) * SLOTS + t]
                    q = jnp.where(s < DEAD, s, 5)
                    prod[q] += res[:, t * CP : (t + 1) * CP]

        rounded = jnp.concatenate([prod[q].astype(jnp.bfloat16) for q in range(5)], axis=1)
        for t in range(SLOTS):
            s = slots[il * SLOTS + t]
            r = parity + s - 2
            mine = (r >= 0) & (r < 2)
            base = jnp.where(mine, r * BAND + shift - r, jnp.where(r == on_row, 22, 27))
            base = jnp.where(s < DEAD, base, 27)
            res = dot_t(tile_at(px, il * SLOTS + t), rounded)
            for q in range(5):
                acc[base + q] += res[:, q * CP : (q + 1) * CP]

    for n in range(22):
        own[n] = acc[n]
    for n in range(5):
        ron[n] = acc[22 + n]


def final_kernel(own, roff, ron, out):
    _, parity = device_id()
    for r in range(2):
        for b in range(BAND):
            out[r, :, b * CP : (b + 1) * CP] = own[r * BAND + b]

    def add(r, b, value):
        cols = pl.ds(pl.multiple_of(b * CP, CP), CP)
        out[r, :, cols] += value

    for p in range(7):
        add(parity, p + 4 * parity, roff[p].astype(jnp.float32))
    for p in range(6):
        add(1 - parity, p + 5 * parity, roff[7 + p].astype(jnp.float32))
    for p in range(5):
        add(1 - parity, p + 6 * (1 - parity), ron[p])


ANY = pl.BlockSpec(memory_space=pl.ANY)
VMEM = pl.BlockSpec(memory_space=pltpu.VMEM)
SMEM = pl.BlockSpec(memory_space=pltpu.SMEM)


def call(kernel, in_specs, out_specs, out_shape, scratch, flops, moved):
    return pl.pallas_call(
        kernel,
        in_specs=in_specs,
        out_specs=out_specs,
        out_shape=out_shape,
        scratch_shapes=scratch,
        compiler_params=pltpu.CompilerParams(vmem_limit_bytes=VMEM_LIMIT),
        cost_estimate=pl.CostEstimate(flops=flops, bytes_accessed=moved, transcendentals=0),
    )


def shape(dims, dtype=jnp.float32):
    return jax.ShapeDtypeStruct(dims, dtype)


def meta_scratch():
    return (pltpu.VMEM((8, CP), jnp.int32), pltpu.SMEM((8, CP), jnp.int32), pltpu.SemaphoreType.DMA((1,)))


def on_device(oper, ocols, ocnt, ptiles, pcols, pcnt):
    size = lax.axis_size(AXES)
    on_pairs = [(i, i ^ 1) for i in range(size)]
    off_pairs = [(i, i + 1) for i in range(1, size - 1, 2)]
    off_pairs += [(j, i) for i, j in off_pairs]
    tiles = ptiles.reshape(2 * PAY_ROWS, CP)
    bf16 = jnp.bfloat16
    dma = pltpu.SemaphoreType.DMA

    pay_on, pay_off = call(
        pack_kernel,
        [SMEM, SMEM, ANY],
        [ANY, ANY],
        [shape((PAY_ROWS + META_ROWS, CP), bf16)] * 2,
        [pltpu.VMEM((2, META_ROWS, CP), bf16), dma((4,))],
        0,
        4 * PAY_ROWS * CP * 2,
    )(pcols, pcnt, tiles)
    got_on = lax.ppermute(pay_on, AXES, on_pairs)
    got_off = lax.ppermute(pay_off, AXES, off_pairs)

    border = call(
        border_kernel,
        [SMEM] * 4 + [ANY, ANY],
        VMEM,
        shape((8 * CP, PANEL), bf16),
        [
            pltpu.VMEM((32, PANEL, PANEL), bf16),
            pltpu.VMEM((PAY_ROWS, CP), bf16),
            pltpu.VMEM((3 * HALF, CP, PANEL), jnp.float32),
            dma((32,)),
            dma((1,)),
        ],
        10 * 2 * PANEL**3,
        2**21,
    )(ocols, ocnt, pcols, pcnt, oper, tiles)
    got_border = lax.ppermute(border, AXES, off_pairs)

    roff, ron1, own1 = call(
        local_kernel,
        [SMEM] * 4 + [ANY, ANY, ANY],
        [VMEM] * 3,
        [shape((13, CP, CP), bf16), shape((15, CP, CP)), shape((22, CP, CP))],
        [
            pltpu.VMEM((8, 8, PANEL, PANEL), bf16),
            pltpu.VMEM((3 * PAY_ROWS, CP), bf16),
            pltpu.VMEM((8, PANEL, CP), jnp.float32),
            pltpu.VMEM((56, CP, CP), jnp.float32),
            pltpu.VMEM((1, META_ROWS, CP), bf16),
            meta_scratch(),
            pltpu.SMEM((64,), jnp.int32),
            dma((8,)),
            dma((3,)),
        ],
        5 * 10**9,
        2**24,
    )(ocols, ocnt, pcols, pcnt, oper, tiles, got_on)
    got_roff = lax.ppermute(roff, AXES, off_pairs)
    got_ron1 = lax.ppermute(ron1, AXES, on_pairs)

    own2, ron2 = call(
        remote_kernel,
        [SMEM] * 4 + [ANY, ANY, ANY, VMEM, VMEM, VMEM],
        [VMEM] * 2,
        [shape((22, CP, CP)), shape((5, CP, CP))],
        [
            pltpu.VMEM((32, PANEL, PANEL), bf16),
            pltpu.VMEM((2 * PAY_ROWS, CP), bf16),
            pltpu.VMEM((6, PANEL, CP), jnp.float32),
            pltpu.VMEM((32, CP, CP), jnp.float32),
            pltpu.VMEM((1, META_ROWS, CP), bf16),
            meta_scratch(),
            pltpu.SMEM((64,), jnp.int32),
            dma((32,)),
            dma((3,)),
        ],
        2 * 10**9,
        2**23,
    )(ocols, ocnt, pcols, pcnt, oper, tiles, got_off, got_border, own1, got_ron1)
    got_ron2 = lax.ppermute(ron2, AXES, on_pairs)

    return call(
        final_kernel,
        [VMEM] * 3,
        VMEM,
        shape((2, CP, BAND * CP)),
        [],
        10**6,
        2**22,
    )(own2, got_roff, got_ron2)


def solution(mesh):
    placed = (
        P(AXES, None, None, None),
        P(AXES, None),
        P(AXES),
        P(AXES, None, None, None),
        P(AXES, None),
        P(AXES),
    )
    return jax.shard_map(
        on_device, mesh=mesh, in_specs=placed, out_specs=P(AXES, None, None), check_vma=False
    )
```

time: 219 us -> 57.2 us (0.26)
  local copies, waits for them, and re-layouts: 111 us -> 2.85 us
  matrix products: 44.2 us -> 0 us
  other arithmetic: 23.7 us -> 0 us
  Pallas kernels: 0 us -> 22.8 us
  waiting for transfers between devices: 22.6 us -> 8.81 us
  starting transfers between devices: 14.9 us -> 21.6 us
    gather x8 -> x0, local copies, waits for them, and re-layouts: 63.7 us -> none  [on_device(): frame_window = frames[jnp.asarray(lookup_table)]]
    dot_general x15 -> x0, matrix products: 44.2 us -> none  [the longest x12 21.8 us: on_device(): jnp.einsum('cdpr,cdrw->cpw', by_offset[:, phase_index, lowest:highest], f...]
    slice x8 -> x0, local copies, waits for them, and re-layouts: 22.8 us -> none  [the longest x4 9.6 us: on_device(): by_offset[:, phase_index, lowest:highest]]
    pallas_call x0 -> x5, Pallas kernels: none -> 22.8 us  [the longest x1 11.5 us: on_device(): call(local_kernel, [SMEM] * 4 + [ANY, ANY, ANY], [VMEM] * 3, [shape((13,...]
    ppermute x4 -> x6, waiting for transfers between devices: 22.6 us -> 8.81 us  [the longest x1 4.92 us: on_device(): got_border = lax.ppermute(border, AXES, off_pairs)]
    scatter-add x4 -> x0, other arithmetic: 10 us -> none  [on_device(): accumulated = accumulated.at[slot_s:slot_s + coarse_local, :, start:start...]
    scatter-add x5 -> x0, local copies, waits for them, and re-layouts: 6.7 us -> none  [the longest x1 6.22 us: on_device(): accumulated = accumulated.at[slot_s:slot_s + coarse_local, :, start:start...]
    ppermute x4 -> x6, starting transfers between devices: 14.9 us -> 21.6 us  [the longest x1 11.1 us: on_device(): got_off = lax.ppermute(pay_off, AXES, off_pairs)]
  transfers between devices with their start and end apart: 4 -> 6, of which waited for: 2 -> 3; matrix products, arithmetic and copies ran while one was open for 18% -> 0% of each run, Pallas kernels for 0% -> 16%
where the time goes in v1:
time: 57.2 us; the launch traced here: 56.1 us
  Pallas kernels  22.8 us (40%)
  starting transfers between devices  21.6 us (38%)
  waiting for transfers between devices  8.81 us (15%)
  local copies, waits for them, and re-layouts  2.85 us (5%)
    pallas_call x1, Pallas kernels, on_device(): call(local_kernel, [SMEM] * 4 + [ANY, ANY, ANY], [VMEM] * 3, [shape((13,...  11.5 us
    ppermute x1, starting transfers between devices, on_device(): got_off = lax.ppermute(pay_off, AXES, off_pairs)  11.1 us
    ppermute x1, starting transfers between devices, on_device(): got_roff = lax.ppermute(roff, AXES, off_pairs)  7.12 us
    pallas_call x1, Pallas kernels, on_device(): call(remote_kernel, [SMEM] * 4 + [ANY, ANY, ANY, VMEM, VMEM, VMEM], [VMEM...  5.95 us
    ppermute x1, waiting for transfers between devices, on_device(): got_border = lax.ppermute(border, AXES, off_pairs)  4.92 us
    pallas_call x1, Pallas kernels, on_device(): call(border_kernel, [SMEM] * 4 + [ANY, ANY], VMEM, shape((8 * CP, PANEL),...  3.2 us
    unnamed x9, local copies, waits for them, and re-layouts  2.85 us
    ppermute x1, starting transfers between devices, on_device(): got_border = lax.ppermute(border, AXES, off_pairs)  2.66 us
  transfers between devices with their start and end apart: 6, of which 3 were waited for; matrix products, arithmetic and copies ran while one was open for 0% of the time, Pallas kernels for 16%

profile of v1, /device:TPU:6, one launch (start us, length us, event | category | flops | bytes accessed | tf_op | source)
XLA Modules:
  0.0 56.1 jit_solution(16694286947393784200)
XLA Ops:
  0.0 0.0 copy-start.3
  0.0 0.0 copy-start.1
  0.0 0.8 %copy.10.columns.pcols = s32[8,3]{1,0:T(8,128)S(1)} copy(s32[8,3]{0,1:T(4,128)} %param.10) | data formatting | bytes 192 | tf_op args[4]
  0.8 0.0 copy-start
  0.8 1.4 %copy-done = bf16[8,3,256,128]{3,2,1,0:T(8,128)(2,1)S(1)} copy-done((bf16[8,3,256,128]{3,2,1,0:T(8,128)(2,1)S(1)}, bf16[8,3,256,128]{3,2,1,0:T(8,128)(2,1)}, u32[]{:S(2)}) %copy-start) | copy-done | bytes 1572888
  2.2 0.0 copy-start.2
  2.2 0.7 %copy-done.2 = s32[8]{0:T(128)S(1)} copy-done((s32[8]{0:T(128)S(1)}, s32[8]{0:T(128)}, u32[]{:S(2)}) %copy-start.2) | copy-done | bytes 56
  2.9 0.8 %shard_map.64 = (bf16[3088,128]{1,0:T(8,128)(2,1)S(1)}, bf16[3088,128]{1,0:T(8,128)(2,1)S(1)}) custom-call(s32[8,3]{1,0:T(8,128)S(1)} %copy.10.columns.pcols, s32[8]{0:T(128)S(1)} %copy-done.2, bf16[6144,128]{1,0:T(8,128)(2,1)S(1)} %bitcast.2), custom_call_target="tpu_custom_call" | custom-call | bytes 3145728 | tf_op jit(solution)/shard_map/pallas_call | solution.py:378
  3.7 0.1 collective-permute-start.2
  3.8 2.3 %collective-permute-done.2.pay = bf16[3088,128]{1,0:T(8,128)(2,1)S(1)} collective-permute-done((bf16[3088,128]{1,0:T(8,128)(2,1)S(1)}, bf16[3088,128]{1,0:T(8,128)(2,1)S(1)}, u32[]{:S(2)}, u32[]{:S(2)}) %collective-permute-start.2) | collective-permute-done | bytes 790560 | tf_op jit(solution)/shard_map/ppermute | solution.py:387
  6.1 0.0 copy-done.3
  6.1 0.0 copy-done.1
  6.1 11.5 %shard_map.66 = (bf16[13,128,128]{2,1,0:T(8,128)(2,1)S(1)}, f32[15,128,128]{2,1,0:T(8,128)S(1)}, f32[22,128,128]{2,1,0:T(8,128)S(1)}) custom-call(s32[8,8]{1,0:T(8,128)S(1)} %copy-done.1, s32[8]{0:T(128)S(1)} %copy-done.3, s32[8,3]{1,0:T(8,128)S(1)} %copy.10.columns.pcols, s32[8]{0:T(128)S(1)} %copy-done.2, bf16[8,8,256,256]{3,2,1,0:T(8,128)(2,1)} %oper.5, ...), custom_call_target="tpu_custom_call" | custom-call | flops 5000000000 | bytes 16777216 | tf_op jit(solution)/shard_map/pallas_call | solution.py:407
  17.6 0.5 collective-permute-start.3
  18.1 11.1 %collective-permute-start = (bf16[3088,128]{1,0:T(8,128)(2,1)S(1)}, bf16[3088,128]{1,0:T(8,128)(2,1)S(1)}, u32[]{:S(2)}, u32[]{:S(2)}) collective-permute-start(bf16[3088,128]{1,0:T(8,128)(2,1)S(1)} %get-tuple-element.12), channel_id=1, source_target_pairs={{1,2},{3,4},{5,6},{7,8},{9,10},{11,12},{13,14},{15,16},{17,18},{19... | collective-permute-start | bytes 2371592 | tf_op jit(solution)/shard_map/ppermute | solution.py:388
  29.2 3.2 %shard_map.65 = bf16[1024,256]{1,0:T(8,128)(2,1)S(1)} custom-call(s32[8,8]{1,0:T(8,128)S(1)} %copy-done.1, s32[8]{0:T(128)S(1)} %copy-done.3, s32[8,3]{1,0:T(8,128)S(1)} %copy.10.columns.pcols, s32[8]{0:T(128)S(1)} %copy-done.2, bf16[8,8,256,256]{3,2,1,0:T(8,128)(2,1)} %oper.5, bf16[6144,128]{1,0:T(8,128)(2,1)S(1)} %bitcast.4), custom_call_target="tpu_custom_call" | custom-call | flops 335544320 | bytes 2097152 | tf_op jit(solution)/shard_map/pallas_call | solution.py:390
  32.4 2.7 %collective-permute-start.1 = (bf16[1024,256]{1,0:T(8,128)(2,1)S(1)}, bf16[1024,256]{1,0:T(8,128)(2,1)S(1)}, u32[]{:S(2)}, u32[]{:S(2)}) collective-permute-start(bf16[1024,256]{1,0:T(8,128)(2,1)S(1)} %shard_map.65), channel_id=1, source_target_pairs={{1,2},{3,4},{5,6},{7,8},{9,10},{11,12},{13,14},{15,16},{17,18},{19... | collective-permute-start | bytes 1572872 | tf_op jit(solution)/shard_map/ppermute | solution.py:405
  35.1 7.1 %collective-permute-start.4 = (bf16[13,128,128]{2,1,0:T(8,128)(2,1)S(1)}, bf16[13,128,128]{2,1,0:T(8,128)(2,1)S(1)}, u32[]{:S(2)}, u32[]{:S(2)}) collective-permute-start(bf16[13,128,128]{2,1,0:T(8,128)(2,1)S(1)} %get-tuple-element.17), channel_id=1, source_target_pairs={{1,2},{3,4},{5,6},{7,8},{9,10},{11,12},{13,14},{15,16},{17,18},{19... | collective-permute-start | bytes 1277960 | tf_op jit(solution)/shard_map/ppermute | solution.py:426
  42.2 4.9 %collective-permute-done.1.bpay = bf16[1024,256]{1,0:T(8,128)(2,1)S(1)} collective-permute-done((bf16[1024,256]{1,0:T(8,128)(2,1)S(1)}, bf16[1024,256]{1,0:T(8,128)(2,1)S(1)}, u32[]{:S(2)}, u32[]{:S(2)}) %collective-permute-start.1) | collective-permute-done | bytes 524320 | tf_op jit(solution)/shard_map/ppermute | solution.py:405
  47.1 0.0 collective-permute-done.pay
  47.1 0.0 collective-permute-done.3.ron1
  47.1 5.9 %shard_map.67 = (f32[22,128,128]{2,1,0:T(8,128)S(1)}, f32[5,128,128]{2,1,0:T(8,128)S(1)}) custom-call(s32[8,8]{1,0:T(8,128)S(1)} %copy-done.1, s32[8]{0:T(128)S(1)} %copy-done.3, s32[8,3]{1,0:T(8,128)S(1)} %copy.10.columns.pcols, s32[8]{0:T(128)S(1)} %copy-done.2, bf16[8,8,256,256]{3,2,1,0:T(8,128)(2,1)} %oper.5, bf16[6144,128]{1,0:T(8,128)(2,1)} %bitcast.1, ...), custom_call_target="tpu_custom_call" | custom-call | flops 2000000000 | bytes 8388608 | tf_op jit(solution)/shard_map/pallas_call | solution.py:429
  53.1 0.1 collective-permute-start.5
  53.2 0.0 collective-permute-done.4.roff
  53.2 1.6 %collective-permute-done.5.ron = f32[5,128,128]{2,1,0:T(8,128)S(1)} collective-permute-done((f32[5,128,128]{2,1,0:T(8,128)S(1)}, f32[5,128,128]{2,1,0:T(8,128)S(1)}, u32[]{:S(2)}, u32[]{:S(2)}) %collective-permute-start.5) | collective-permute-done | bytes 327712 | tf_op jit(solution)/shard_map/ppermute | solution.py:448
  54.8 1.3 %shard_map.68 = f32[2,128,1408]{2,1,0:T(8,128)} custom-call(f32[22,128,128]{2,1,0:T(8,128)S(1)} %get-tuple-element.16.own, bf16[13,128,128]{2,1,0:T(8,128)(2,1)S(1)} %collective-permute-done.4.roff, f32[5,128,128]{2,1,0:T(8,128)S(1)} %collective-permute-done.5.ron), custom_call_target="tpu_custom_call" | custom-call | flops 1000000 | bytes 4194304 | tf_op jit(solution)/shard_map/pallas_call | solution.py:450
Async XLA Ops:
  0.0 6.1 %copy-start.3 = (s32[8]{0:T(128)S(1)}, s32[8]{0:T(128)}, u32[]{:S(2)}) copy-start(s32[8]{0:T(128)} %ocnt.5) | copy-start | bytes 100
  0.0 6.1 %copy-start.1 = (s32[8,8]{1,0:T(8,128)S(1)}, s32[8,8]{1,0:T(8,128)}, u32[]{:S(2)}) copy-start(s32[8,8]{1,0:T(8,128)} %ocols.5) | copy-start | bytes 772
  0.8 1.4 %copy-start = (bf16[8,3,256,128]{3,2,1,0:T(8,128)(2,1)S(1)}, bf16[8,3,256,128]{3,2,1,0:T(8,128)(2,1)}, u32[]{:S(2)}) copy-start(bf16[8,3,256,128]{3,2,1,0:T(8,128)(2,1)} %param.9) | copy-start | bytes 4718596
  2.2 0.7 %copy-start.2 = (s32[8]{0:T(128)S(1)}, s32[8]{0:T(128)}, u32[]{:S(2)}) copy-start(s32[8]{0:T(128)} %pcnt.5) | copy-start | bytes 100
  3.7 2.4 %collective-permute-start.2 = (bf16[3088,128]{1,0:T(8,128)(2,1)S(1)}, bf16[3088,128]{1,0:T(8,128)(2,1)S(1)}, u32[]{:S(2)}, u32[]{:S(2)}) collective-permute-start(bf16[3088,128]{1,0:T(8,128)(2,1)S(1)} %get-tuple-element.13), channel_id=1, source_target_pairs={{0,1},{1,0},{2,3},{3,2},{4,5},{5,4},{6,7},{7,6},{8,9},{9,8},{10,11... | collective-permute-start | bytes 2371592 | tf_op jit(solution)/shard_map/ppermute | solution.py:387
  17.6 29.6 %collective-permute-start.3 = (f32[15,128,128]{2,1,0:T(8,128)S(1)}, f32[15,128,128]{2,1,0:T(8,128)S(1)}, u32[]{:S(2)}, u32[]{:S(2)}) collective-permute-start(f32[15,128,128]{2,1,0:T(8,128)S(1)} %get-tuple-element.15), channel_id=1, source_target_pairs={{0,1},{1,0},{2,3},{3,2},{4,5},{5,4},{6,7},{7,6},{8,9},{9,8},{10,11... | collective-permute-start | bytes 2949128 | tf_op jit(solution)/shard_map/ppermute | solution.py:427
  18.1 29.1 %collective-permute-start = (bf16[3088,128]{1,0:T(8,128)(2,1)S(1)}, bf16[3088,128]{1,0:T(8,128)(2,1)S(1)}, u32[]{:S(2)}, u32[]{:S(2)}) collective-permute-start(bf16[3088,128]{1,0:T(8,128)(2,1)S(1)} %get-tuple-element.12), channel_id=1, source_target_pairs={{1,2},{3,4},{5,6},{7,8},{9,10},{11,12},{13,14},{15,16},{17,18},{19... | collective-permute-start | bytes 2371592 | tf_op jit(solution)/shard_map/ppermute | solution.py:388
  32.4 14.7 %collective-permute-start.1 = (bf16[1024,256]{1,0:T(8,128)(2,1)S(1)}, bf16[1024,256]{1,0:T(8,128)(2,1)S(1)}, u32[]{:S(2)}, u32[]{:S(2)}) collective-permute-start(bf16[1024,256]{1,0:T(8,128)(2,1)S(1)} %shard_map.65), channel_id=1, source_target_pairs={{1,2},{3,4},{5,6},{7,8},{9,10},{11,12},{13,14},{15,16},{17,18},{19... | collective-permute-start | bytes 1572872 | tf_op jit(solution)/shard_map/ppermute | solution.py:405
  35.1 18.1 %collective-permute-start.4 = (bf16[13,128,128]{2,1,0:T(8,128)(2,1)S(1)}, bf16[13,128,128]{2,1,0:T(8,128)(2,1)S(1)}, u32[]{:S(2)}, u32[]{:S(2)}) collective-permute-start(bf16[13,128,128]{2,1,0:T(8,128)(2,1)S(1)} %get-tuple-element.17), channel_id=1, source_target_pairs={{1,2},{3,4},{5,6},{7,8},{9,10},{11,12},{13,14},{15,16},{17,18},{19... | collective-permute-start | bytes 1277960 | tf_op jit(solution)/shard_map/ppermute | solution.py:426
  53.1 1.7 %collective-permute-start.5 = (f32[5,128,128]{2,1,0:T(8,128)S(1)}, f32[5,128,128]{2,1,0:T(8,128)S(1)}, u32[]{:S(2)}, u32[]{:S(2)}) collective-permute-start(f32[5,128,128]{2,1,0:T(8,128)S(1)} %get-tuple-element.18), channel_id=1, source_target_pairs={{0,1},{1,0},{2,3},{3,2},{4,5},{5,4},{6,7},{7,6},{8,9},{9,8},{10,11... | collective-permute-start | bytes 983048 | tf_op jit(solution)/shard_map/ppermute | solution.py:448

commit v2 on v0

v2 whole, which is shorter than its diff:
```python
import jax
import jax.numpy as jnp
from jax import lax
from jax.experimental import pallas as pl
from jax.experimental.pallas import tpu as pltpu
from jax.sharding import PartitionSpec as P

AXES = ("row", "grp")
PANEL = 256
CP = 128
HALF = 4
SLOTS = 3
BAND = 11
DEAD = 7
TILE3 = SLOTS * CP
PAY = HALF * TILE3
META = 16
VMEM_LIMIT = 48 * 1024 * 1024
UNROLL = 12
F32 = jnp.float32
BF16 = jnp.bfloat16


def device_id():
    grp = lax.axis_index("grp")
    return lax.axis_index("row") * lax.axis_size("grp") + grp, lax.rem(grp, 2)


def slot_of(columns, counts, device, panel, slot):
    s = columns[slot, panel] - (2 * device + lax.div(panel, HALF)) + 2
    return jnp.where(slot < counts[panel], s, DEAD)


def rows_at(ref, start, size, step=CP):
    return ref[pl.ds(pl.multiple_of(start, step), size), :]


def dot(a, b):
    return jnp.dot(a, b, preferred_element_type=F32)


def dot_nt(a, b):
    return lax.dot_general(a, b, (((1,), (1,)), ((), ())), preferred_element_type=F32)


def off_hits(ocols, ocnt, device, parity, hits):
    found = 0
    for il in range(HALF):
        i = parity * HALF + il
        for k in range(1, 8):
            j = ocols[i, k] - 8 * device
            jo = jnp.where(parity == 1, j - 8, j + HALF)
            hits[found] = il * 64 + k * 8 + jo
            found += ((k < ocnt[i]) & (jo >= 0) & (jo < HALF)).astype(jnp.int32)
    return found


def field(code, shift, bits):
    return (code >> shift) & (2**bits - 1)


def clear(ref, count):
    @pl.loop(0, count)
    def _(n):
        ref[n] = jnp.zeros(ref.shape[1:], F32)


def first_kernel(
    ocols_h, ocnt_h, pcols_h, pcnt_h, oper, tiles, pt, on_ref, off_ref, abuf,
    raw, ocols, ocnt, pcols, pcnt, acc, hits, sems, asem,
):
    device, parity = device_id()
    halves = ((off_ref, parity), (on_ref, 1 - parity))
    copies = [
        pltpu.make_async_copy(tiles.at[pl.ds(half * HALF * SLOTS, HALF * SLOTS)], raw.at[at], sems.at[at])
        for at, (_, half) in enumerate(halves)
    ]
    small = [
        pltpu.make_async_copy(src, dst, sems.at[2 + at])
        for at, (src, dst) in enumerate(((ocols_h, ocols), (ocnt_h, ocnt), (pcols_h, pcols), (pcnt_h, pcnt)))
    ]
    for copy in small + copies:
        copy.start()
    for copy in small:
        copy.wait()
    count = off_hits(ocols, ocnt, device, parity, hits)

    def a_copy(n):
        code = hits[n]
        return pltpu.make_async_copy(
            oper.at[parity * HALF + field(code, 6, 2), field(code, 3, 3)], abuf.at[n], asem.at[n]
        )

    @pl.loop(0, count)
    def _(n):
        a_copy(n).start()

    lane = lax.broadcasted_iota(jnp.int32, (META, PANEL), 1)
    for ref, half in halves:
        values = jnp.zeros((META, PANEL), jnp.int32)
        for p in range(HALF):
            for t in range(SLOTS):
                s = slot_of(pcols, pcnt, device, half * HALF + p, t)
                values = jnp.where(lane == p * SLOTS + t, s, values)
        ref[PAY : PAY + META, :] = values.astype(F32).astype(BF16)
    for n in range(2 * HALF):
        acc[n] = jnp.zeros((CP, PANEL), F32)
    for at, (ref, half) in enumerate(halves):
        copies[at].wait()
        for n in range(HALF * SLOTS):
            turned = raw[at, n].T
            ref[n * CP : (n + 1) * CP, :] = turned
            pt[pl.ds(pl.multiple_of(half * PAY + n * CP, CP), CP), :] = turned

    @pl.loop(0, count)
    def _(n):
        a_copy(n).wait()

    @pl.loop(0, lax.div(count + 3, 4))
    def _(block):
        for u in range(4):
            n = block * 4 + u
            code = hits[n]
            il, jo = field(code, 6, 2), field(code, 0, 2)
            res = dot(rows_at(off_ref, (il * SLOTS + 1) * CP, 2 * CP), abuf[n])
            for t in range(1, SLOTS):
                s = slot_of(pcols, pcnt, device, parity * HALF + il, t)
                near = s == jnp.where(parity == 1, 3, 1)
                far = s == jnp.where(parity == 1, 4, 0)
                at = jnp.where(near, jo * 2, jnp.where(far, jo * 2 + 1, 8))
                acc[jnp.where(n < count, at, 8)] += res[(t - 1) * CP : t * CP]

    for n in range(2 * HALF):
        off_ref[PAY + META + n * CP : PAY + META + (n + 1) * CP, :] = acc[n].astype(BF16)


def read_meta(pay, vec, smem, sem, slots, at):
    vec[...] = pay[PAY : PAY + META, :].astype(F32).astype(jnp.int32)
    copy = pltpu.make_async_copy(vec, smem, sem)
    copy.start()
    copy.wait()
    for n in range(HALF * SLOTS):
        slots[at + n] = smem[0, n]


def local_kernel(
    ocols, ocnt, pcols, pcnt, oper, pt, pay, roff, ron, own,
    abuf, px, prod, acc, vec, smem, slots, hits, asem, psem,
):
    device, parity = device_id()
    on = 1 - parity
    copies = [
        pltpu.make_async_copy(pt, px.at[pl.ds(0, 2 * PAY)], psem.at[0]),
        pltpu.make_async_copy(pay.at[pl.ds(0, PAY)], px.at[pl.ds(2 * PAY, PAY)], psem.at[1]),
    ]
    for copy in copies:
        copy.start()

    def a_copy(n):
        code = hits[n]
        return pltpu.make_async_copy(oper.at[field(code, 9, 3), field(code, 6, 3)], abuf.at[n], asem.at[n])

    count = 0
    for i in range(8):
        began = count
        for k in range(8):
            j = ocols[i, k] - 8 * device
            mine = (j >= 0) & (j < 8)
            jn = jnp.where(parity == 1, j + HALF, j - 8)
            theirs = (jn >= 0) & (jn < HALF)
            x = jnp.where(mine, j, 8 + jn)
            base = ((j + 8) >> 2) - 1 - i // HALF
            hits[count] = i * 512 + k * 64 + x * 4 + base
            count += ((k < ocnt[i]) & (mine | theirs)).astype(jnp.int32)

        @pl.loop(began, count)
        def _(n):
            a_copy(n).start()

    for i in range(8):
        for t in range(SLOTS):
            slots[i * SLOTS + t] = slot_of(pcols, pcnt, device, i, t)
    read_meta(pay, vec, smem, psem.at[2], slots, 8 * SLOTS)
    clear(prod, 64)
    clear(acc, 48)
    for copy in copies:
        copy.wait()

    @pl.loop(0, count)
    def _(n):
        a_copy(n).wait()

    @pl.loop(0, lax.div(count + UNROLL - 1, UNROLL))
    def _(block):
        for u in range(UNROLL):
            n = jnp.minimum(block * UNROLL + u, count - 1)
            code = hits[n]
            i, x, base = field(code, 9, 3), field(code, 2, 4), field(code, 0, 2)
            base = jnp.where(block * UNROLL + u < count, i * 8 + base, 64)
            res = dot_nt(rows_at(px, x * TILE3, TILE3), abuf[n])
            for t in range(SLOTS):
                s = slots[x * SLOTS + t]
                prod[jnp.where(s < DEAD, base + s, 64)] += res[t * CP : (t + 1) * CP]

    @pl.loop(0, 2)
    def _(m):
        for p in range(HALF):
            i = m * HALF + p
            lhs = rows_at(px, i * TILE3, TILE3)
            at = []
            for t in range(SLOTS):
                s = slots[i * SLOTS + t]
                at.append(jnp.where(s < DEAD, m + s, 6) * 8 + m)
            for q0 in range(0, 7, 2):
                wide = min(2, 7 - q0)
                rhs = jnp.concatenate([prod[i * 8 + q0 + w].astype(BF16) for w in range(wide)], axis=0)
                res = dot_nt(lhs, rhs)
                for t in range(SLOTS):
                    for w in range(wide):
                        acc[at[t] + q0 + w] += res[t * CP : (t + 1) * CP, w * CP : (w + 1) * CP]

    near_off = jnp.where(parity == 1, 4, 1)
    far_off = jnp.where(parity == 1, 5, 0)
    for p in range(7):
        roff[p] = acc[near_off * 8 + p + on].astype(BF16)
    for p in range(6):
        roff[7 + p] = acc[far_off * 8 + p + 1].astype(BF16)
    near_on = jnp.where(parity == 1, 1, 4)
    far_on = jnp.where(parity == 1, 0, 5)
    for p in range(8):
        ron[p] = acc[near_on * 8 + p].astype(BF16)
    for p in range(7):
        ron[8 + p] = acc[far_on * 8 + p + on].astype(BF16)
    for r in range(2):
        for b in range(BAND):
            cb = b - 2 + r
            if 0 <= cb < 8:
                own[r * BAND + b] = acc[(r + 2) * 8 + cb]
            else:
                own[r * BAND + b] = jnp.zeros((CP, CP), F32)


def merge_kernel(own1, ron1, own):
    _, parity = device_id()
    on = 1 - parity
    for n in range(22):
        own[n] = own1[n]
    for p in range(8):
        own[on * BAND + p + 3 * on] += ron1[p].astype(F32)
    for p in range(7):
        own[parity * BAND + p + 4 * on] += ron1[8 + p].astype(F32)


def remote_kernel(
    ocols, ocnt, pcols, pcnt, abuf, pt, pay, own1, own, ron, prod, acc, vec, smem, slots, hits, psem
):
    device, parity = device_id()
    vec[...] = pay[PAY : PAY + META, :].astype(F32).astype(jnp.int32)
    meta = pltpu.make_async_copy(vec, smem, psem.at[0])
    meta.start()
    count = off_hits(ocols, ocnt, device, parity, hits)
    for il in range(HALF):
        for t in range(SLOTS):
            slots[il * SLOTS + t] = slot_of(pcols, pcnt, device, parity * HALF + il, t)
    clear(prod, HALF * 6)
    for n in range(22):
        acc[n] = own1[n]
    for n in range(22, 27):
        acc[n] = jnp.zeros((CP, CP), F32)
    meta.wait()

    @pl.loop(0, lax.div(count + 3, 4))
    def _(block):
        for u in range(4):
            n = jnp.minimum(block * 4 + u, count - 1)
            code = hits[n]
            il, jo = field(code, 6, 2), field(code, 0, 2)
            res = dot_nt(rows_at(pay, jo * TILE3, TILE3), abuf[n])
            for t in range(SLOTS):
                s = smem[0, jo * SLOTS + t]
                live = (s < DEAD) & (block * 4 + u < count)
                prod[jnp.where(live, il * 6 + s, 5)] += res[t * CP : (t + 1) * CP]

    on_row = jnp.where(parity == 1, -1, 2)
    shift = jnp.where(parity == 1, 5, 2)
    for il in range(HALF):
        lhs = rows_at(pt, (parity * HALF + il) * TILE3, TILE3)
        b_at = PAY + META + il * 2 * CP
        b_res = dot_nt(pay[b_at : b_at + 2 * CP, :], lhs)
        at = []
        for t in range(SLOTS):
            s = slots[il * SLOTS + t]
            r = parity + s - 2
            mine = (r >= 0) & (r < 2)
            base = jnp.where(mine, r * BAND + shift - r, jnp.where(r == on_row, 22, 27))
            at.append(jnp.where(s < DEAD, base, 27))
            for near in range(2):
                r = parity if near == 0 else 1 - parity
                b_row = jnp.where(s < DEAD, r * BAND + parity + s + 3 - r, 27)
                acc[b_row] += b_res[near * CP : (near + 1) * CP, t * CP : (t + 1) * CP]
        for q0 in range(0, 5, 2):
            wide = min(2, 5 - q0)
            rhs = jnp.concatenate([prod[il * 6 + q0 + w].astype(BF16) for w in range(wide)], axis=0)
            res = dot_nt(lhs, rhs)
            for t in range(SLOTS):
                for w in range(wide):
                    acc[at[t] + q0 + w] += res[t * CP : (t + 1) * CP, w * CP : (w + 1) * CP]

    for n in range(22):
        own[n] = acc[n]
    for n in range(5):
        ron[n] = acc[22 + n]


def final_kernel(own, roff, ron, out):
    _, parity = device_id()
    on = 1 - parity
    for r in range(2):
        for b in range(BAND):
            out[r, :, b * CP : (b + 1) * CP] = own[r * BAND + b]

    def add(r, b, value):
        cols = pl.ds(pl.multiple_of(b * CP, CP), CP)
        out[r, :, cols] += value

    for p in range(7):
        add(parity, p + 4 * parity, roff[p].astype(F32))
    for p in range(6):
        add(on, p + 5 * parity, roff[7 + p].astype(F32))
    for p in range(5):
        add(on, p + 6 * on, ron[p])


ANY = pl.BlockSpec(memory_space=pl.ANY)
HBM = pl.BlockSpec(memory_space=pltpu.HBM)
VMEM = pl.BlockSpec(memory_space=pltpu.VMEM)
SMEM = pl.BlockSpec(memory_space=pltpu.SMEM)


def call(kernel, in_specs, out_specs, out_shape, scratch):
    return pl.pallas_call(
        kernel,
        in_specs=in_specs,
        out_specs=out_specs,
        out_shape=out_shape,
        scratch_shapes=scratch,
        compiler_params=pltpu.CompilerParams(vmem_limit_bytes=VMEM_LIMIT),
        cost_estimate=pl.CostEstimate(flops=1000, bytes_accessed=1000, transcendentals=0),
    )


def shape(dims, dtype=F32):
    return jax.ShapeDtypeStruct(dims, dtype)


def on_device(oper, ocols, ocnt, ptiles, pcols, pcnt):
    size = lax.axis_size(AXES)
    on_pairs = [(i, i ^ 1) for i in range(size)]
    off_pairs = [(i, i + 1) for i in range(1, size - 1, 2)]
    off_pairs += [(j, i) for i, j in off_pairs]
    tiles = ptiles.reshape(8 * SLOTS, PANEL, CP)
    pcols = pcols.T
    dma = pltpu.SemaphoreType.DMA
    i32 = jnp.int32
    meta = [pltpu.VMEM((META, PANEL), i32), pltpu.SMEM((META, PANEL), i32), pltpu.SMEM((64,), i32)]

    pt, pay_on, pay_off, edge = call(
        first_kernel,
        [HBM] * 6,
        [VMEM] * 4,
        [
            shape((2 * PAY, PANEL), BF16),
            shape((PAY + META, PANEL), BF16),
            shape((PAY + META + 8 * CP, PANEL), BF16),
            shape((12, PANEL, PANEL), BF16),
        ],
        [
            pltpu.VMEM((2, HALF * SLOTS, PANEL, CP), BF16),
            pltpu.SMEM((8, 8), i32),
            pltpu.SMEM((8,), i32),
            pltpu.SMEM((SLOTS, 8), i32),
            pltpu.SMEM((8,), i32),
            pltpu.VMEM((9, CP, PANEL), F32),
            pltpu.SMEM((32,), i32),
            dma((6,)),
            dma((12,)),
        ],
    )(ocols, ocnt, pcols, pcnt, oper, tiles)
    got_on = lax.ppermute(pay_on, AXES, on_pairs)
    got_off = lax.ppermute(pay_off, AXES, off_pairs)

    roff, ron1, own1 = call(
        local_kernel,
        [SMEM] * 4 + [HBM, VMEM, VMEM],
        [VMEM] * 3,
        [shape((13, CP, CP), BF16), shape((15, CP, CP), BF16), shape((22, CP, CP))],
        [
            pltpu.VMEM((64, PANEL, PANEL), BF16),
            pltpu.VMEM((3 * PAY, PANEL), BF16),
            pltpu.VMEM((65 + 7, CP, PANEL), F32),
            pltpu.VMEM((56, CP, CP), F32),
            *meta,
            pltpu.SMEM((72,), i32),
            dma((64,)),
            dma((3,)),
        ],
    )(ocols, ocnt, pcols, pcnt, oper, pt, got_on)
    got_roff = lax.ppermute(roff, AXES, off_pairs)
    got_ron1 = lax.ppermute(ron1, AXES, on_pairs)
    own1 = call(merge_kernel, [VMEM] * 2, VMEM, shape((22, CP, CP)), [])(own1, got_ron1)

    own2, ron2 = call(
        remote_kernel,
        [SMEM] * 4 + [VMEM] * 4,
        [VMEM] * 2,
        [shape((22, CP, CP)), shape((5, CP, CP))],
        [
            pltpu.VMEM((HALF * 6, CP, PANEL), F32),
            pltpu.VMEM((32, CP, CP), F32),
            *meta,
            pltpu.SMEM((32,), i32),
            dma((1,)),
        ],
    )(ocols, ocnt, pcols, pcnt, edge, pt, got_off, own1)
    got_ron2 = lax.ppermute(ron2, AXES, on_pairs)

    return call(final_kernel, [VMEM] * 3, VMEM, shape((2, CP, BAND * CP)), [])(own2, got_roff, got_ron2)


def solution(mesh):
    placed = (
        P(AXES, None, None, None),
        P(AXES, None),
        P(AXES),
        P(AXES, None, None, None),
        P(AXES, None),
        P(AXES),
    )
    return jax.shard_map(
        on_device, mesh=mesh, in_specs=placed, out_specs=P(AXES, None, None), check_vma=False
    )
```

time: 219 us -> 41.4 us (0.19)
  local copies, waits for them, and re-layouts: 111 us -> 2.68 us
  matrix products: 44.2 us -> 0 us
  other arithmetic: 23.7 us -> 0 us
  Pallas kernels: 0 us -> 17.3 us
  waiting for transfers between devices: 22.6 us -> 8.13 us
  starting transfers between devices: 14.9 us -> 12.5 us
    gather x8 -> x0, local copies, waits for them, and re-layouts: 63.7 us -> none  [on_device(): frame_window = frames[jnp.asarray(lookup_table)]]
    dot_general x15 -> x0, matrix products: 44.2 us -> none  [the longest x12 21.8 us: on_device(): jnp.einsum('cdpr,cdrw->cpw', by_offset[:, phase_index, lowest:highest], f...]
    slice x8 -> x0, local copies, waits for them, and re-layouts: 22.8 us -> none  [the longest x4 9.6 us: on_device(): by_offset[:, phase_index, lowest:highest]]
    pallas_call x0 -> x5, Pallas kernels: none -> 17.3 us  [the longest x1 9.32 us: on_device(): call(local_kernel, [SMEM] * 4 + [HBM, VMEM, VMEM], [VMEM] * 3, [shape((13...]
    ppermute x4 -> x5, waiting for transfers between devices: 22.6 us -> 8.13 us  [the longest x1 5.84 us: on_device(): got_roff = lax.ppermute(roff, AXES, off_pairs)]
    scatter-add x4 -> x0, other arithmetic: 10 us -> none  [on_device(): accumulated = accumulated.at[slot_s:slot_s + coarse_local, :, start:start...]
    scatter-add x5 -> x0, local copies, waits for them, and re-layouts: 6.7 us -> none  [the longest x1 6.22 us: on_device(): accumulated = accumulated.at[slot_s:slot_s + coarse_local, :, start:start...]
    convert_element_type x1 -> x0, local copies, waits for them, and re-layouts: 6.22 us -> none  [expand_frames(): frame.reshape(tiles.shape[0], tiles.shape[2], PFRAME * tiles.shape[3])]
  transfers between devices with their start and end apart: 4 -> 5, of which waited for: 2 -> 2; matrix products, arithmetic and copies ran while one was open for 18% -> 0% of each run, Pallas kernels for 0% -> 33%
where the time goes in v2:
time: 41.4 us; the launch traced here: 40.7 us
  Pallas kernels  17.3 us (42%)
  starting transfers between devices  12.5 us (30%)
  waiting for transfers between devices  8.13 us (20%)
  local copies, waits for them, and re-layouts  2.68 us (6%)
    pallas_call x1, Pallas kernels, on_device(): call(local_kernel, [SMEM] * 4 + [HBM, VMEM, VMEM], [VMEM] * 3, [shape((13...  9.32 us
    ppermute x1, starting transfers between devices, on_device(): got_off = lax.ppermute(pay_off, AXES, off_pairs)  8.54 us
    ppermute x1, waiting for transfers between devices, on_device(): got_roff = lax.ppermute(roff, AXES, off_pairs)  5.84 us
    pallas_call x1, Pallas kernels, on_device(): call(remote_kernel, [SMEM] * 4 + [VMEM] * 4, [VMEM] * 2, [shape((22, CP,...  3.97 us
    ppermute x1, starting transfers between devices, on_device(): got_roff = lax.ppermute(roff, AXES, off_pairs)  3.52 us
    unnamed x10, local copies, waits for them, and re-layouts  2.68 us
    pallas_call x1, Pallas kernels, on_device(): call(first_kernel, [HBM] * 6, [VMEM] * 4, [shape((2 * PAY, PANEL), BF16),...  2.46 us
    ppermute x1, waiting for transfers between devices, on_device(): got_on = lax.ppermute(pay_on, AXES, on_pairs)  2.28 us
  transfers between devices with their start and end apart: 5, of which 2 were waited for; matrix products, arithmetic and copies ran while one was open for 0% of the time, Pallas kernels for 33%

profile of v2, /device:TPU:6, one launch (start us, length us, event | category | flops | bytes accessed | tf_op | source)
XLA Modules:
  0.0 40.7 jit_solution(11342994064237042354)
XLA Ops:
  0.0 0.0 copy-start.1
  0.0 0.7 %copy-done.1 = s32[8,8]{1,0:T(8,128)S(1)} copy-done((s32[8,8]{1,0:T(8,128)S(1)}, s32[8,8]{1,0:T(8,128)}, u32[]{:S(2)}) %copy-start.1) | copy-done | bytes 280
  0.7 0.0 copy-start.2
  0.7 0.7 %copy-done.2 = s32[8,3]{0,1:T(4,128)S(1)} copy-done((s32[8,3]{0,1:T(4,128)S(1)}, s32[8,3]{0,1:T(4,128)}, u32[]{:S(2)}) %copy-start.2) | copy-done | bytes 120
  1.4 0.0 copy-start.3
  1.4 0.7 %copy-done.3 = s32[8]{0:T(128)S(1)} copy-done((s32[8]{0:T(128)S(1)}, s32[8]{0:T(128)}, u32[]{:S(2)}) %copy-start.3) | copy-done | bytes 56
  2.0 0.0 copy-start.4
  2.0 0.7 %copy-done.4 = s32[8]{0:T(128)S(1)} copy-done((s32[8]{0:T(128)S(1)}, s32[8]{0:T(128)}, u32[]{:S(2)}) %copy-start.4) | copy-done | bytes 56
  2.7 2.5 %shard_map.64 = (bf16[3072,256]{1,0:T(8,128)(2,1)S(1)}, bf16[1552,256]{1,0:T(8,128)(2,1)S(1)}, bf16[2576,256]{1,0:T(8,128)(2,1)S(1)}, bf16[12,256,256]{2,1,0:T(8,128)(2,1)S(1)}) custom-call(s32[8,8]{1,0:T(8,128)S(1)} %copy-done.1, s32[8]{0:T(128)S(1)} %copy-done.3, s32[3,8]{1,0:T(4,128)S(1)} %bitcast.2, s32[8]{0:T(128)S(1)} %copy-done.4, ...), custom_call_target="tpu_custom_call" | custom-call | flops 1000 | bytes 1000 | tf_op jit(solution)/shard_map/pallas_call | solution.py:367
  5.2 0.0 copy-start
  5.2 8.5 %collective-permute-start = (bf16[2576,256]{1,0:T(8,128)(2,1)S(1)}, bf16[2576,256]{1,0:T(8,128)(2,1)S(1)}, u32[]{:S(2)}, u32[]{:S(2)}) collective-permute-start(bf16[2576,256]{1,0:T(8,128)(2,1)S(1)} %get-tuple-element.16), channel_id=1, source_target_pairs={{1,2},{3,4},{5,6},{7,8},{9,10},{11,12},{13,14},{15,16},{17,18},{19... | collective-permute-start | bytes 3956744 | tf_op jit(solution)/shard_map/ppermute | solution.py:390
  13.7 0.1 collective-permute-start.1
  13.8 2.3 %collective-permute-done.1.pay = bf16[1552,256]{1,0:T(8,128)(2,1)S(1)} collective-permute-done((bf16[1552,256]{1,0:T(8,128)(2,1)S(1)}, bf16[1552,256]{1,0:T(8,128)(2,1)S(1)}, u32[]{:S(2)}, u32[]{:S(2)}) %collective-permute-start.1) | collective-permute-done | bytes 794656 | tf_op jit(solution)/shard_map/ppermute | solution.py:389
  16.1 9.3 %shard_map.65 = (bf16[13,128,128]{2,1,0:T(8,128)(2,1)S(1)}, bf16[15,128,128]{2,1,0:T(8,128)(2,1)S(1)}, f32[22,128,128]{2,1,0:T(8,128)S(1)}) custom-call(s32[8,8]{1,0:T(8,128)S(1)} %copy-done.1, s32[8]{0:T(128)S(1)} %copy-done.3, s32[3,8]{1,0:T(4,128)S(1)} %bitcast.3, s32[8]{0:T(128)S(1)} %copy-done.4, bf16[8,8,256,256]{3,2,1,0:T(8,128)(2,1)} %oper.3, ...), custom_call_target="tpu_custom_call" | custom-call | flops 1000 | bytes 1000 | tf_op jit(solution)/shard_map/pallas_call | solution.py:392
  25.4 0.0 copy-done
  25.4 0.3 collective-permute-start.2
  25.7 3.5 %collective-permute-start.3 = (bf16[13,128,128]{2,1,0:T(8,128)(2,1)S(1)}, bf16[13,128,128]{2,1,0:T(8,128)(2,1)S(1)}, u32[]{:S(2)}, u32[]{:S(2)}) collective-permute-start(bf16[13,128,128]{2,1,0:T(8,128)(2,1)S(1)} %get-tuple-element.21), channel_id=1, source_target_pairs={{1,2},{3,4},{5,6},{7,8},{9,10},{11,12},{13,14},{15,16},{17,18},{19... | collective-permute-start | bytes 1277960 | tf_op jit(solution)/shard_map/ppermute | solution.py:408
  29.2 0.0 collective-permute-done.2.ron1
  29.2 0.2 shard_map.66.own1
  29.4 0.0 collective-permute-done.pay
  29.4 4.0 %shard_map.67 = (f32[22,128,128]{2,1,0:T(8,128)S(1)}, f32[5,128,128]{2,1,0:T(8,128)S(1)}) custom-call(s32[8,8]{1,0:T(8,128)S(1)} %copy-done.1, s32[8]{0:T(128)S(1)} %copy-done.3, s32[3,8]{1,0:T(4,128)S(1)} %bitcast.4, s32[8]{0:T(128)S(1)} %copy-done.4, bf16[12,256,256]{2,1,0:T(8,128)(2,1)S(1)} %get-tuple-element.14.abuf, bf16[3072,256]{1,0:T(8,128)(2,1)} %copy-done, ...), custom_call_target="tpu_custom_call" | custom-call | flops 1000 | bytes 1000 | tf_op jit(solution)/shard_map/pallas_call | solution.py:412
  33.4 0.1 collective-permute-start.4
  33.5 5.8 %collective-permute-done.3.roff = bf16[13,128,128]{2,1,0:T(8,128)(2,1)S(1)} collective-permute-done((bf16[13,128,128]{2,1,0:T(8,128)(2,1)S(1)}, bf16[13,128,128]{2,1,0:T(8,128)(2,1)S(1)}, u32[]{:S(2)}, u32[]{:S(2)}) %collective-permute-start.3) | collective-permute-done | bytes 426016 | tf_op jit(solution)/shard_map/ppermute | solution.py:408
  39.4 0.0 collective-permute-done.4.ron
  39.4 1.3 %shard_map.68 = f32[2,128,1408]{2,1,0:T(8,128)} custom-call(f32[22,128,128]{2,1,0:T(8,128)S(1)} %get-tuple-element.20.own, bf16[13,128,128]{2,1,0:T(8,128)(2,1)S(1)} %collective-permute-done.3.roff, f32[5,128,128]{2,1,0:T(8,128)S(1)} %collective-permute-done.4.ron), custom_call_target="tpu_custom_call" | custom-call | flops 1000 | bytes 1000 | tf_op jit(solution)/shard_map/pallas_call | solution.py:427
Async XLA Ops:
  0.0 0.7 %copy-start.1 = (s32[8,8]{1,0:T(8,128)S(1)}, s32[8,8]{1,0:T(8,128)}, u32[]{:S(2)}) copy-start(s32[8,8]{1,0:T(8,128)} %ocols.3) | copy-start | bytes 772
  0.7 0.7 %copy-start.2 = (s32[8,3]{0,1:T(4,128)S(1)}, s32[8,3]{0,1:T(4,128)}, u32[]{:S(2)}) copy-start(s32[8,3]{0,1:T(4,128)} %param.10) | copy-start | bytes 292
  1.4 0.7 %copy-start.3 = (s32[8]{0:T(128)S(1)}, s32[8]{0:T(128)}, u32[]{:S(2)}) copy-start(s32[8]{0:T(128)} %ocnt.3) | copy-start | bytes 100
  2.0 0.7 %copy-start.4 = (s32[8]{0:T(128)S(1)}, s32[8]{0:T(128)}, u32[]{:S(2)}) copy-start(s32[8]{0:T(128)} %pcnt.3) | copy-start | bytes 100
  5.2 20.3 %copy-start = (bf16[3072,256]{1,0:T(8,128)(2,1)}, bf16[3072,256]{1,0:T(8,128)(2,1)S(1)}, u32[]{:S(2)}) copy-start(bf16[3072,256]{1,0:T(8,128)(2,1)S(1)} %get-tuple-element.15.pt) | copy-start | bytes 4718596
  5.2 24.3 %collective-permute-start = (bf16[2576,256]{1,0:T(8,128)(2,1)S(1)}, bf16[2576,256]{1,0:T(8,128)(2,1)S(1)}, u32[]{:S(2)}, u32[]{:S(2)}) collective-permute-start(bf16[2576,256]{1,0:T(8,128)(2,1)S(1)} %get-tuple-element.16), channel_id=1, source_target_pairs={{1,2},{3,4},{5,6},{7,8},{9,10},{11,12},{13,14},{15,16},{17,18},{19... | collective-permute-start | bytes 3956744 | tf_op jit(solution)/shard_map/ppermute | solution.py:390
  13.7 2.4 %collective-permute-start.1 = (bf16[1552,256]{1,0:T(8,128)(2,1)S(1)}, bf16[1552,256]{1,0:T(8,128)(2,1)S(1)}, u32[]{:S(2)}, u32[]{:S(2)}) collective-permute-start(bf16[1552,256]{1,0:T(8,128)(2,1)S(1)} %get-tuple-element.17), channel_id=1, source_target_pairs={{0,1},{1,0},{2,3},{3,2},{4,5},{5,4},{6,7},{7,6},{8,9},{9,8},{10,11... | collective-permute-start | bytes 2383880 | tf_op jit(solution)/shard_map/ppermute | solution.py:389
  25.4 3.8 %collective-permute-start.2 = (bf16[15,128,128]{2,1,0:T(8,128)(2,1)S(1)}, bf16[15,128,128]{2,1,0:T(8,128)(2,1)S(1)}, u32[]{:S(2)}, u32[]{:S(2)}) collective-permute-start(bf16[15,128,128]{2,1,0:T(8,128)(2,1)S(1)} %get-tuple-element.19), channel_id=1, source_target_pairs={{0,1},{1,0},{2,3},{3,2},{4,5},{5,4},{6,7},{7,6},{8,9},{9,8},{10,11... | collective-permute-start | bytes 1474568 | tf_op jit(solution)/shard_map/ppermute | solution.py:409
  25.7 13.7 %collective-permute-start.3 = (bf16[13,128,128]{2,1,0:T(8,128)(2,1)S(1)}, bf16[13,128,128]{2,1,0:T(8,128)(2,1)S(1)}, u32[]{:S(2)}, u32[]{:S(2)}) collective-permute-start(bf16[13,128,128]{2,1,0:T(8,128)(2,1)S(1)} %get-tuple-element.21), channel_id=1, source_target_pairs={{1,2},{3,4},{5,6},{7,8},{9,10},{11,12},{13,14},{15,16},{17,18},{19... | collective-permute-start | bytes 1277960 | tf_op jit(solution)/shard_map/ppermute | solution.py:408
  33.4 5.9 %collective-permute-start.4 = (f32[5,128,128]{2,1,0:T(8,128)S(1)}, f32[5,128,128]{2,1,0:T(8,128)S(1)}, u32[]{:S(2)}, u32[]{:S(2)}) collective-permute-start(f32[5,128,128]{2,1,0:T(8,128)S(1)} %get-tuple-element.22), channel_id=1, source_target_pairs={{0,1},{1,0},{2,3},{3,2},{4,5},{5,4},{6,7},{7,6},{8,9},{9,8},{10,11... | collective-permute-start | bytes 983048 | tf_op jit(solution)/shard_map/ppermute | solution.py:425

commit v3 on v2

v3 whole, which is shorter than its diff:
```python
import jax
import jax.numpy as jnp
from jax import lax
from jax.experimental import pallas as pl
from jax.experimental.pallas import tpu as pltpu
from jax.sharding import PartitionSpec as P

AXES = ("row", "grp")
PANEL = 256
CP = 128
HALF = 4
SLOTS = 3
BAND = 11
DEAD = 7
TILE3 = SLOTS * CP
PAY = HALF * TILE3
META = 16
VMEM_LIMIT = 45 * 1024 * 1024
UNROLL = 12
PCOLS, OCNT, PCNT = 8, 11, 12
F32 = jnp.float32
BF16 = jnp.bfloat16


def device_id():
    grp = lax.axis_index("grp")
    return lax.axis_index("row") * lax.axis_size("grp") + grp, lax.rem(grp, 2)


def slot_of(table, device, panel, slot):
    s = table[PCOLS + slot, panel] - (2 * device + lax.div(panel, HALF)) + 2
    return jnp.where(slot < table[PCNT, panel], s, DEAD)


def rows_at(ref, start, size, step=CP):
    return ref[pl.ds(pl.multiple_of(start, step), size), :]


def dot(a, b):
    return jnp.dot(a, b, preferred_element_type=F32)


def dot_nt(a, b):
    return lax.dot_general(a, b, (((1,), (1,)), ((), ())), preferred_element_type=F32)


def off_hits(table, device, parity, hits):
    found = 0
    for il in range(HALF):
        i = parity * HALF + il
        live = table[OCNT, i]
        columns = [table[i, k] for k in range(1, 8)]
        for k, j in enumerate(columns, 1):
            jo = j - 8 * device + jnp.where(parity == 1, -8, HALF)
            hits[found] = il * 64 + k * 8 + jo
            found += ((k < live) & (jo >= 0) & (jo < HALF)).astype(jnp.int32)
    return found


def field(code, shift, bits):
    return (code >> shift) & (2**bits - 1)


def clear(ref, count):
    @pl.loop(0, count)
    def _(n):
        ref[n] = jnp.zeros(ref.shape[1:], F32)


def first_kernel(table, oper, tiles, pt, out, abuf, raw, acc, hits, sems, asem):
    device, parity = device_id()
    copies = [
        pltpu.make_async_copy(tiles.at[pl.ds(half * HALF * SLOTS, HALF * SLOTS)], raw.at[at], sems.at[at])
        for at, half in enumerate((parity, 1 - parity))
    ]
    for copy in copies:
        copy.start()
    count = off_hits(table, device, parity, hits)

    def a_copy(n):
        code = hits[n]
        return pltpu.make_async_copy(
            oper.at[parity * HALF + field(code, 6, 2), field(code, 3, 3)], abuf.at[n], asem.at[n]
        )

    @pl.loop(0, count)
    def _(n):
        a_copy(n).start()

    lane = lax.broadcasted_iota(jnp.int32, (META, PANEL), 1)
    for ref, at, half in ((out, PAY, parity), (pt, 2 * PAY, 1 - parity)):
        values = jnp.zeros((META, PANEL), jnp.int32)
        for p in range(HALF):
            for t in range(SLOTS):
                s = slot_of(table, device, half * HALF + p, t)
                values = jnp.where(lane == p * SLOTS + t, s, values)
        ref[at : at + META, :] = values.astype(F32).astype(BF16)
    for n in range(2 * HALF):
        acc[n] = jnp.zeros((CP, PANEL), F32)
    for at, half in enumerate((parity, 1 - parity)):
        copies[at].wait()
        for n in range(HALF * SLOTS):
            turned = raw[at, n].T
            pt[pl.ds(pl.multiple_of(half * PAY + n * CP, CP), CP), :] = turned
            if at == 0:
                out[n * CP : (n + 1) * CP, :] = turned

    @pl.loop(0, count)
    def _(n):
        a_copy(n).wait()

    @pl.loop(0, lax.div(count + 3, 4))
    def _(block):
        for u in range(4):
            n = block * 4 + u
            code = hits[n]
            il, jo = field(code, 6, 2), field(code, 0, 2)
            res = dot(rows_at(out, (il * SLOTS + 1) * CP, 2 * CP), abuf[n])
            for t in range(1, SLOTS):
                s = slot_of(table, device, parity * HALF + il, t)
                near = s == jnp.where(parity == 1, 3, 1)
                far = s == jnp.where(parity == 1, 4, 0)
                at = jnp.where(near, jo * 2, jnp.where(far, jo * 2 + 1, 8))
                acc[jnp.where(n < count, at, 8)] += res[(t - 1) * CP : t * CP]

    for n in range(2 * HALF):
        out[PAY + META + n * CP : PAY + META + (n + 1) * CP, :] = acc[n].astype(BF16)


def local_kernel(
    table, oper, pt, got, roff, ron_near, ron_far, own, abuf, px, prod, acc, vec, smem, slots, hits, asem, psem
):
    device, parity = device_id()
    on = 1 - parity
    vec[...] = got[2 * PAY :, :CP].astype(F32).astype(jnp.int32)[:1]
    meta = pltpu.make_async_copy(vec, smem, psem.at[2])
    copies = [
        pltpu.make_async_copy(pt.at[pl.ds(0, 2 * PAY)], px.at[pl.ds(0, 2 * PAY)], psem.at[0]),
        pltpu.make_async_copy(
            got.at[pl.ds(pl.multiple_of(parity * PAY, PAY), PAY)], px.at[pl.ds(2 * PAY, PAY)], psem.at[1]
        ),
    ]
    meta.start()
    for copy in copies:
        copy.start()

    def a_copy(n):
        code = hits[n]
        return pltpu.make_async_copy(oper.at[field(code, 9, 3), field(code, 6, 3)], abuf.at[n], asem.at[n])

    count = 0
    for i in range(8):
        began = count
        live = table[OCNT, i]
        columns = [table[i, k] for k in range(8)]
        for k, column in enumerate(columns):
            j = column - 8 * device
            mine = (j >= 0) & (j < 8)
            jn = j + jnp.where(parity == 1, HALF, -8)
            theirs = (jn >= 0) & (jn < HALF)
            x = jnp.where(mine, j, 8 + jn)
            base = ((j + 8) >> 2) - 1 - i // HALF
            hits[count] = i * 512 + k * 64 + x * 4 + base
            count += ((k < live) & (mine | theirs)).astype(jnp.int32)

        @pl.loop(began, count)
        def _(n):
            a_copy(n).start()

    for t in range(SLOTS):
        own_slots = [slot_of(table, device, i, t) for i in range(8)]
        for i in range(8):
            slots[i * SLOTS + t] = own_slots[i]
    clear(prod, 64)
    clear(acc, 48)
    meta.wait()
    their_slots = [smem[0, n] for n in range(HALF * SLOTS)]
    for n in range(HALF * SLOTS):
        slots[8 * SLOTS + n] = their_slots[n]
    for copy in copies:
        copy.wait()

    @pl.loop(0, lax.div(count + UNROLL - 1, UNROLL))
    def _(block):
        @pl.loop(block * UNROLL, jnp.minimum(block * UNROLL + UNROLL, count))
        def _(n):
            a_copy(n).wait()

        for u in range(UNROLL):
            n = jnp.minimum(block * UNROLL + u, count - 1)
            code = hits[n]
            i, x, base = field(code, 9, 3), field(code, 2, 4), field(code, 0, 2)
            base = jnp.where(block * UNROLL + u < count, i * 8 + base, 64)
            res = dot_nt(rows_at(px, x * TILE3, TILE3), abuf[n])
            for t in range(SLOTS):
                s = slots[x * SLOTS + t]
                prod[jnp.where(s < DEAD, base + s, 64)] += res[t * CP : (t + 1) * CP]

    @pl.loop(0, 2)
    def _(m):
        for p in range(HALF):
            i = m * HALF + p
            lhs = rows_at(px, i * TILE3, TILE3)
            at = []
            for t in range(SLOTS):
                s = slots[i * SLOTS + t]
                at.append(jnp.where(s < DEAD, m + s, 6) * 8 + m)
            for q0 in range(0, 7, 2):
                wide = min(2, 7 - q0)
                rhs = jnp.concatenate([prod[i * 8 + q0 + w].astype(BF16) for w in range(wide)], axis=0)
                res = dot_nt(lhs, rhs)
                for t in range(SLOTS):
                    for w in range(wide):
                        acc[at[t] + q0 + w] += res[t * CP : (t + 1) * CP, w * CP : (w + 1) * CP]

    near = jnp.where(parity == 1, 4, 1)
    far = jnp.where(parity == 1, 5, 0)
    for p in range(7):
        roff[p] = acc[near * 8 + p + on].astype(BF16)
    for p in range(6):
        roff[7 + p] = acc[far * 8 + p + 1].astype(BF16)
    near = jnp.where(parity == 1, 1, 4)
    far = jnp.where(parity == 1, 0, 5)
    for p in range(8):
        ron_near[p] = acc[near * 8 + p].astype(BF16)
    for p in range(7):
        ron_far[p] = acc[far * 8 + p + on].astype(BF16)
    for r in range(2):
        for b in range(BAND):
            cb = b - 2 + r
            if 0 <= cb < 8:
                own[r * BAND + b] = acc[(r + 2) * 8 + cb]
            else:
                own[r * BAND + b] = jnp.zeros((CP, CP), F32)


def remote_kernel(
    table, abuf, pt, pay, own1, own, ron, prod, acc, vec, smem, slots, hits, psem
):
    device, parity = device_id()
    vec[...] = pay[PAY : PAY + META, :CP].astype(F32).astype(jnp.int32)[:1]
    meta = pltpu.make_async_copy(vec, smem, psem.at[0])
    meta.start()
    count = off_hits(table, device, parity, hits)
    for il in range(HALF):
        for t in range(SLOTS):
            slots[il * SLOTS + t] = slot_of(table, device, parity * HALF + il, t)
    clear(prod, HALF * 6)
    for n in range(22):
        acc[n] = own1[n]
    for n in range(22, 27):
        acc[n] = jnp.zeros((CP, CP), F32)
    meta.wait()

    @pl.loop(0, lax.div(count + 3, 4))
    def _(block):
        for u in range(4):
            n = jnp.minimum(block * 4 + u, count - 1)
            code = hits[n]
            il, jo = field(code, 6, 2), field(code, 0, 2)
            res = dot_nt(rows_at(pay, jo * TILE3, TILE3), abuf[n])
            for t in range(SLOTS):
                s = smem[0, jo * SLOTS + t]
                live = (s < DEAD) & (block * 4 + u < count)
                prod[jnp.where(live, il * 6 + s, 5)] += res[t * CP : (t + 1) * CP]

    on_row = jnp.where(parity == 1, -1, 2)
    shift = jnp.where(parity == 1, 5, 2)
    for il in range(HALF):
        lhs = rows_at(pt, (parity * HALF + il) * TILE3, TILE3)
        b_at = PAY + META + il * 2 * CP
        b_res = dot_nt(pay[b_at : b_at + 2 * CP, :], lhs)
        at = []
        for t in range(SLOTS):
            s = slots[il * SLOTS + t]
            r = parity + s - 2
            mine = (r >= 0) & (r < 2)
            base = jnp.where(mine, r * BAND + shift - r, jnp.where(r == on_row, 22, 27))
            at.append(jnp.where(s < DEAD, base, 27))
            for near in range(2):
                r = parity if near == 0 else 1 - parity
                b_row = jnp.where(s < DEAD, r * BAND + parity + s + 3 - r, 27)
                acc[b_row] += b_res[near * CP : (near + 1) * CP, t * CP : (t + 1) * CP]
        for q0 in range(0, 5, 2):
            wide = min(2, 5 - q0)
            rhs = jnp.concatenate([prod[il * 6 + q0 + w].astype(BF16) for w in range(wide)], axis=0)
            res = dot_nt(lhs, rhs)
            for t in range(SLOTS):
                for w in range(wide):
                    acc[at[t] + q0 + w] += res[t * CP : (t + 1) * CP, w * CP : (w + 1) * CP]

    for n in range(22):
        own[n] = acc[n]
    for n in range(5):
        ron[n] = acc[22 + n].astype(BF16)


def final_kernel(own, roff, near, far, ron, out):
    _, parity = device_id()
    on = 1 - parity
    for r in range(2):
        for b in range(BAND):
            out[r, :, b * CP : (b + 1) * CP] = own[r * BAND + b]

    def add(r, b, value):
        cols = pl.ds(pl.multiple_of(b * CP, CP), CP)
        out[r, :, cols] += value

    for p in range(7):
        add(parity, p + 4 * parity, roff[p].astype(F32))
    for p in range(6):
        add(on, p + 5 * parity, roff[7 + p].astype(F32))
    for p in range(5):
        add(on, p + 6 * on, ron[p].astype(F32))
    for p in range(8):
        add(on, p + 3 * on, near[p].astype(F32))
    for p in range(7):
        add(parity, p + 4 * on, far[p].astype(F32))


ANY = pl.BlockSpec(memory_space=pl.ANY)
HBM = pl.BlockSpec(memory_space=pltpu.HBM)
VMEM = pl.BlockSpec(memory_space=pltpu.VMEM)
SMEM = pl.BlockSpec(memory_space=pltpu.SMEM)


def call(kernel, in_specs, out_specs, out_shape, scratch):
    return pl.pallas_call(
        kernel,
        in_specs=in_specs,
        out_specs=out_specs,
        out_shape=out_shape,
        scratch_shapes=scratch,
        compiler_params=pltpu.CompilerParams(vmem_limit_bytes=VMEM_LIMIT),
        cost_estimate=pl.CostEstimate(flops=1000, bytes_accessed=1000, transcendentals=0),
    )


def shape(dims, dtype=F32):
    return jax.ShapeDtypeStruct(dims, dtype)


def on_device(oper, ocols, ocnt, ptiles, pcols, pcnt):
    size = lax.axis_size(AXES)
    on_pairs = [(i, i ^ 1) for i in range(size)]
    off_pairs = [(i, i + 1) for i in range(1, size - 1, 2)]
    off_pairs += [(j, i) for i, j in off_pairs]
    tiles = ptiles.reshape(8 * SLOTS, PANEL, CP)
    dma = pltpu.SemaphoreType.DMA
    i32 = jnp.int32
    meta = [pltpu.VMEM((1, CP), i32), pltpu.SMEM((1, CP), i32), pltpu.SMEM((64,), i32)]

    table = jnp.concatenate([ocols, pcols.T, ocnt[None], pcnt[None]])
    pt, pay_off, edge = call(
        first_kernel,
        [SMEM, HBM, HBM],
        [VMEM] * 3,
        [
            shape((2 * PAY + META, PANEL), BF16),
            shape((PAY + META + 8 * CP, PANEL), BF16),
            shape((12, PANEL, PANEL), BF16),
        ],
        [
            pltpu.VMEM((2, HALF * SLOTS, PANEL, CP), BF16),
            pltpu.VMEM((9, CP, PANEL), F32),
            pltpu.SMEM((32,), i32),
            dma((2,)),
            dma((12,)),
        ],
    )(table, oper, tiles)
    got_on = lax.ppermute(pt, AXES, on_pairs)
    got_off = lax.ppermute(pay_off, AXES, off_pairs)

    roff, near, far, own1 = call(
        local_kernel,
        [SMEM, HBM, VMEM, VMEM],
        [VMEM] * 4,
        [shape((13, CP, CP), BF16), shape((8, CP, CP), BF16), shape((7, CP, CP), BF16), shape((22, CP, CP))],
        [
            pltpu.VMEM((64, PANEL, PANEL), BF16),
            pltpu.VMEM((3 * PAY, PANEL), BF16),
            pltpu.VMEM((72, CP, PANEL), F32),
            pltpu.VMEM((56, CP, CP), F32),
            *meta,
            pltpu.SMEM((72,), i32),
            dma((64,)),
            dma((3,)),
        ],
    )(table, oper, pt, got_on)
    got_roff = lax.ppermute(roff, AXES, off_pairs)
    got_near = lax.ppermute(near, AXES, on_pairs)
    got_far = lax.ppermute(far, AXES, on_pairs)

    own2, ron2 = call(
        remote_kernel,
        [SMEM] + [VMEM] * 4,
        [VMEM] * 2,
        [shape((22, CP, CP)), shape((5, CP, CP), BF16)],
        [
            pltpu.VMEM((HALF * 6, CP, PANEL), F32),
            pltpu.VMEM((32, CP, CP), F32),
            *meta,
            pltpu.SMEM((32,), i32),
            dma((1,)),
        ],
    )(table, edge, pt, got_off, own1)
    got_ron2 = lax.ppermute(ron2, AXES, on_pairs)

    return call(final_kernel, [VMEM] * 5, VMEM, shape((2, CP, BAND * CP)), [])(
        own2, got_roff, got_near, got_far, got_ron2
    )


def solution(mesh):
    placed = (
        P(AXES, None, None, None),
        P(AXES, None),
        P(AXES),
        P(AXES, None, None, None),
        P(AXES, None),
        P(AXES),
    )
    return jax.shard_map(
        on_device, mesh=mesh, in_specs=placed, out_specs=P(AXES, None, None), check_vma=False
    )
```

time: 41.4 us -> 37.9 us (0.915); the launches traced: 40.7 us -> 37.7 us
  waiting for transfers between devices: 8.13 us -> 6.47 us
  local copies, waits for them, and re-layouts: 2.68 us -> 1.4 us
  Pallas kernels: 17.3 us -> 16.4 us
  other arithmetic: 0 us -> 0.74 us
    ppermute x1, waiting for transfers between devices: 5.84 us -> 2 us  [on_device(): got_roff = lax.ppermute(roff, AXES, off_pairs)]
    ppermute x1, waiting for transfers between devices: 0.01 us -> 3.08 us  [on_device(): got_off = lax.ppermute(pay_off, AXES, off_pairs)]
    ppermute x2 -> x3, waiting for transfers between devices: 2.29 us -> 0.01 us  [the longest x1 0.01 us: on_device(): got_far = lax.ppermute(far, AXES, on_pairs)]
    ppermute x1, waiting for transfers between devices: 0.01 us -> 1.38 us  [on_device(): got_ron2 = lax.ppermute(ron2, AXES, on_pairs)]
    unnamed x10 -> x2, local copies, waits for them, and re-layouts: 2.68 us -> 1.4 us
    pallas_call x5 -> x4, Pallas kernels: 17.3 us -> 16.4 us  [the longest x1 8.63 us: on_device(): call(local_kernel, [SMEM, HBM, VMEM, VMEM], [VMEM] * 4, [shape((13, CP, C...]
    concatenate x0 -> x1, other arithmetic: none -> 0.74 us  [on_device(): table = jnp.concatenate([ocols, pcols.T, ocnt[None], pcnt[None]])]
    ppermute x1, starting transfers between devices: 3.52 us -> 3.04 us  [on_device(): got_roff = lax.ppermute(roff, AXES, off_pairs)]
  transfers between devices with their start and end apart: 5 -> 6, of which waited for: 2 -> 3; matrix products, arithmetic and copies ran while one was open for 0% -> 0% of each run, Pallas kernels for 33% -> 32%
where the time goes in v3:
time: 37.9 us; the launch traced here: 37.7 us
  Pallas kernels  16.4 us (43%)
  starting transfers between devices  12.6 us (33%)
  waiting for transfers between devices  6.47 us (17%)
  local copies, waits for them, and re-layouts  1.4 us (4%)
  other arithmetic  0.74 us (2%)
    ppermute x1, starting transfers between devices, on_device(): got_off = lax.ppermute(pay_off, AXES, off_pairs)  8.8 us
    pallas_call x1, Pallas kernels, on_device(): call(local_kernel, [SMEM, HBM, VMEM, VMEM], [VMEM] * 4, [shape((13, CP, C...  8.63 us
    pallas_call x1, Pallas kernels, on_device(): call(remote_kernel, [SMEM] + [VMEM] * 4, [VMEM] * 2, [shape((22, CP, CP))...  3.46 us
    ppermute x1, waiting for transfers between devices, on_device(): got_off = lax.ppermute(pay_off, AXES, off_pairs)  3.08 us
    ppermute x1, starting transfers between devices, on_device(): got_roff = lax.ppermute(roff, AXES, off_pairs)  3.04 us
    pallas_call x1, Pallas kernels, on_device(): call(first_kernel, [SMEM, HBM, HBM], [VMEM] * 3, [shape((2 * PAY + META,...  2.91 us
    ppermute x1, waiting for transfers between devices, on_device(): got_roff = lax.ppermute(roff, AXES, off_pairs)  2 us
    pallas_call x1, Pallas kernels, on_device(): call(final_kernel, [VMEM] * 5, VMEM, shape((2, CP, BAND * CP)), [])  1.44 us
  transfers between devices with their start and end apart: 6, of which 3 were waited for; matrix products, arithmetic and copies ran while one was open for 0% of the time, Pallas kernels for 32%

profile of v3, /device:TPU:6, one launch (start us, length us, event | category | flops | bytes accessed | tf_op | source)
XLA Modules:
  0.0 37.7 jit_solution(4394363367849442383)
XLA Ops:
  0.0 0.7 %pad_add_fusion.table = s32[13,8]{1,0:T(8,128)S(1)} fusion(s32[1,8]{1,0:T(1,128)} %bitcast.6, s32[1,8]{1,0:T(1,128)} %bitcast.7, s32[3,8]{1,0:T(4,128)} %bitcast.5, s32[8,8]{1,0:T(8,128)} %param.7), kind=kLoop, calls=%fused_computation | loop fusion | flops 312 | bytes 832 | tf_op jit(solution)/shard_map/concatenate | solution.py:353
  0.7 0.0 copy-start
  0.8 1.4 %copy-done = bf16[8,3,256,128]{3,2,1,0:T(8,128)(2,1)S(1)} copy-done((bf16[8,3,256,128]{3,2,1,0:T(8,128)(2,1)S(1)}, bf16[8,3,256,128]{3,2,1,0:T(8,128)(2,1)}, u32[]{:S(2)}) %copy-start) | copy-done | bytes 1572888
  2.2 2.9 %shard_map.64 = (bf16[3088,256]{1,0:T(8,128)(2,1)S(1)}, bf16[2576,256]{1,0:T(8,128)(2,1)S(1)}, bf16[12,256,256]{2,1,0:T(8,128)(2,1)S(1)}) custom-call(s32[13,8]{1,0:T(8,128)S(1)} %pad_add_fusion.table, bf16[8,8,256,256]{3,2,1,0:T(8,128)(2,1)} %oper.3, bf16[24,256,128]{2,1,0:T(8,128)(2,1)S(1)} %bitcast.4), custom_call_target="tpu_custom_call" | custom-call | flops 1000 | bytes 1000 | tf_op jit(solution)/shard_map/pallas_call | solution.py:354
  5.1 0.1 collective-permute-start.1
  5.2 8.8 %collective-permute-start = (bf16[2576,256]{1,0:T(8,128)(2,1)S(1)}, bf16[2576,256]{1,0:T(8,128)(2,1)S(1)}, u32[]{:S(2)}, u32[]{:S(2)}) collective-permute-start(bf16[2576,256]{1,0:T(8,128)(2,1)S(1)} %get-tuple-element.16), channel_id=1, source_target_pairs={{1,2},{3,4},{5,6},{7,8},{9,10},{11,12},{13,14},{15,16},{17,18},{19... | collective-permute-start | bytes 3956744 | tf_op jit(solution)/shard_map/ppermute | solution.py:372
  14.0 0.0 collective-permute-done.1.got
  14.0 8.6 %shard_map.65 = (bf16[13,128,128]{2,1,0:T(8,128)(2,1)S(1)}, bf16[8,128,128]{2,1,0:T(8,128)(2,1)S(1)}, bf16[7,128,128]{2,1,0:T(8,128)(2,1)S(1)}, f32[22,128,128]{2,1,0:T(8,128)S(1)}) custom-call(s32[13,8]{1,0:T(8,128)S(1)} %pad_add_fusion.table, bf16[8,8,256,256]{3,2,1,0:T(8,128)(2,1)} %oper.3, bf16[3088,256]{1,0:T(8,128)(2,1)S(1)} %get-tuple-element.15.pt, ...), custom_call_target="tpu_custom_call" | custom-call | flops 1000 | bytes 1000 | tf_op jit(solution)/shard_map/pallas_call | solution.py:374
  22.6 3.0 %collective-permute-start.2 = (bf16[13,128,128]{2,1,0:T(8,128)(2,1)S(1)}, bf16[13,128,128]{2,1,0:T(8,128)(2,1)S(1)}, u32[]{:S(2)}, u32[]{:S(2)}) collective-permute-start(bf16[13,128,128]{2,1,0:T(8,128)(2,1)S(1)} %get-tuple-element.19), channel_id=1, source_target_pairs={{1,2},{3,4},{5,6},{7,8},{9,10},{11,12},{13,14},{15,16},{17,18},{19... | collective-permute-start | bytes 1277960 | tf_op jit(solution)/shard_map/ppermute | solution.py:390
  25.7 0.1 collective-permute-start.3
  25.8 0.5 %collective-permute-start.4 = (bf16[7,128,128]{2,1,0:T(8,128)(2,1)S(1)}, bf16[7,128,128]{2,1,0:T(8,128)(2,1)S(1)}, u32[]{:S(2)}, u32[]{:S(2)}) collective-permute-start(bf16[7,128,128]{2,1,0:T(8,128)(2,1)S(1)} %get-tuple-element.21), channel_id=1, source_target_pairs={{0,1},{1,0},{2,3},{3,2},{4,5},{5,4},{6,7},{7,6},{8,9},{9,8},{10,11... | collective-permute-start | bytes 688136 | tf_op jit(solution)/shard_map/ppermute | solution.py:392
  26.3 3.1 %collective-permute-done.pay = bf16[2576,256]{1,0:T(8,128)(2,1)S(1)} collective-permute-done((bf16[2576,256]{1,0:T(8,128)(2,1)S(1)}, bf16[2576,256]{1,0:T(8,128)(2,1)S(1)}, u32[]{:S(2)}, u32[]{:S(2)}) %collective-permute-start) | collective-permute-done | bytes 1318944 | tf_op jit(solution)/shard_map/ppermute | solution.py:372
  29.3 3.5 %shard_map.66 = (f32[22,128,128]{2,1,0:T(8,128)S(1)}, bf16[5,128,128]{2,1,0:T(8,128)(2,1)S(1)}) custom-call(s32[13,8]{1,0:T(8,128)S(1)} %pad_add_fusion.table, bf16[12,256,256]{2,1,0:T(8,128)(2,1)S(1)} %get-tuple-element.14.abuf, bf16[3088,256]{1,0:T(8,128)(2,1)S(1)} %get-tuple-element.15.pt, bf16[2576,256]{1,0:T(8,128)(2,1)S(1)} %collective-permute-done.pay, ...), custom_call_target="tpu_custom_call" | custom-call | flops 1000 | bytes 1000 | tf_op jit(solution)/shard_map/pallas_call | solution.py:394
  32.8 0.1 collective-permute-start.5
  32.9 1.4 %collective-permute-done.5.ron = bf16[5,128,128]{2,1,0:T(8,128)(2,1)S(1)} collective-permute-done((bf16[5,128,128]{2,1,0:T(8,128)(2,1)S(1)}, bf16[5,128,128]{2,1,0:T(8,128)(2,1)S(1)}, u32[]{:S(2)}, u32[]{:S(2)}) %collective-permute-start.5) | collective-permute-done | bytes 163872 | tf_op jit(solution)/shard_map/ppermute | solution.py:407
  34.3 0.0 collective-permute-done.4.far
  34.3 0.0 collective-permute-done.3.near
  34.3 2.0 %collective-permute-done.2.roff = bf16[13,128,128]{2,1,0:T(8,128)(2,1)S(1)} collective-permute-done((bf16[13,128,128]{2,1,0:T(8,128)(2,1)S(1)}, bf16[13,128,128]{2,1,0:T(8,128)(2,1)S(1)}, u32[]{:S(2)}, u32[]{:S(2)}) %collective-permute-start.2) | collective-permute-done | bytes 426016 | tf_op jit(solution)/shard_map/ppermute | solution.py:390
  36.3 1.4 %shard_map.67 = f32[2,128,1408]{2,1,0:T(8,128)} custom-call(f32[22,128,128]{2,1,0:T(8,128)S(1)} %get-tuple-element.18.own, bf16[13,128,128]{2,1,0:T(8,128)(2,1)S(1)} %collective-permute-done.2.roff, bf16[8,128,128]{2,1,0:T(8,128)(2,1)S(1)} %collective-permute-done.3.near, bf16[7,128,128]{2,1,0:T(8,128)(2,1)S(1)} %collective-permute-done.4.far, ...), custom_call_target="tpu_custom_call" | custom-call | flops 1000 | bytes 1000 | tf_op jit(solution)/shard_map/pallas_call | solution.py:409
Async XLA Ops:
  0.7 1.4 %copy-start = (bf16[8,3,256,128]{3,2,1,0:T(8,128)(2,1)S(1)}, bf16[8,3,256,128]{3,2,1,0:T(8,128)(2,1)}, u32[]{:S(2)}) copy-start(bf16[8,3,256,128]{3,2,1,0:T(8,128)(2,1)} %param.9) | copy-start | bytes 4718596
  5.1 8.9 %collective-permute-start.1 = (bf16[3088,256]{1,0:T(8,128)(2,1)S(1)}, bf16[3088,256]{1,0:T(8,128)(2,1)S(1)}, u32[]{:S(2)}, u32[]{:S(2)}) collective-permute-start(bf16[3088,256]{1,0:T(8,128)(2,1)S(1)} %get-tuple-element.15.pt), channel_id=1, source_target_pairs={{0,1},{1,0},{2,3},{3,2},{4,5},{5,4},{6,7},{7,6},{8,9},{9,8},{10,11... | collective-permute-start | bytes 4743176 | tf_op jit(solution)/shard_map/ppermute | solution.py:371
  5.2 24.2 %collective-permute-start = (bf16[2576,256]{1,0:T(8,128)(2,1)S(1)}, bf16[2576,256]{1,0:T(8,128)(2,1)S(1)}, u32[]{:S(2)}, u32[]{:S(2)}) collective-permute-start(bf16[2576,256]{1,0:T(8,128)(2,1)S(1)} %get-tuple-element.16), channel_id=1, source_target_pairs={{1,2},{3,4},{5,6},{7,8},{9,10},{11,12},{13,14},{15,16},{17,18},{19... | collective-permute-start | bytes 3956744 | tf_op jit(solution)/shard_map/ppermute | solution.py:372
  22.6 13.7 %collective-permute-start.2 = (bf16[13,128,128]{2,1,0:T(8,128)(2,1)S(1)}, bf16[13,128,128]{2,1,0:T(8,128)(2,1)S(1)}, u32[]{:S(2)}, u32[]{:S(2)}) collective-permute-start(bf16[13,128,128]{2,1,0:T(8,128)(2,1)S(1)} %get-tuple-element.19), channel_id=1, source_target_pairs={{1,2},{3,4},{5,6},{7,8},{9,10},{11,12},{13,14},{15,16},{17,18},{19... | collective-permute-start | bytes 1277960 | tf_op jit(solution)/shard_map/ppermute | solution.py:390
  25.7 8.6 %collective-permute-start.3 = (bf16[8,128,128]{2,1,0:T(8,128)(2,1)S(1)}, bf16[8,128,128]{2,1,0:T(8,128)(2,1)S(1)}, u32[]{:S(2)}, u32[]{:S(2)}) collective-permute-start(bf16[8,128,128]{2,1,0:T(8,128)(2,1)S(1)} %get-tuple-element.20), channel_id=1, source_target_pairs={{0,1},{1,0},{2,3},{3,2},{4,5},{5,4},{6,7},{7,6},{8,9},{9,8},{10,11... | collective-permute-start | bytes 786440 | tf_op jit(solution)/shard_map/ppermute | solution.py:391
  25.8 8.5 %collective-permute-start.4 = (bf16[7,128,128]{2,1,0:T(8,128)(2,1)S(1)}, bf16[7,128,128]{2,1,0:T(8,128)(2,1)S(1)}, u32[]{:S(2)}, u32[]{:S(2)}) collective-permute-start(bf16[7,128,128]{2,1,0:T(8,128)(2,1)S(1)} %get-tuple-element.21), channel_id=1, source_target_pairs={{0,1},{1,0},{2,3},{3,2},{4,5},{5,4},{6,7},{7,6},{8,9},{9,8},{10,11... | collective-permute-start | bytes 688136 | tf_op jit(solution)/shard_map/ppermute | solution.py:392
  32.8 1.5 %collective-permute-start.5 = (bf16[5,128,128]{2,1,0:T(8,128)(2,1)S(1)}, bf16[5,128,128]{2,1,0:T(8,128)(2,1)S(1)}, u32[]{:S(2)}, u32[]{:S(2)}) collective-permute-start(bf16[5,128,128]{2,1,0:T(8,128)(2,1)S(1)} %get-tuple-element.22), channel_id=1, source_target_pairs={{0,1},{1,0},{2,3},{3,2},{4,5},{5,4},{6,7},{7,6},{8,9},{9,8},{10,11... | collective-permute-start | bytes 491528 | tf_op jit(solution)/shard_map/ppermute | solution.py:407

commit v4 on v3

--- a/solution.py
+++ b/solution.py
@@ -196,8 +196,7 @@
                 s = slots[x * SLOTS + t]
                 prod[jnp.where(s < DEAD, base + s, 64)] += res[t * CP : (t + 1) * CP]
 
-    @pl.loop(0, 2)
-    def _(m):
+    for m in range(2):
         for p in range(HALF):
             i = m * HALF + p
             lhs = rows_at(px, i * TILE3, TILE3)

time: 37.9 us -> 37.9 us (level)
  Pallas kernels: 16.4 us -> 15.5 us
  waiting for transfers between devices: 6.47 us -> 6.95 us
  starting transfers between devices: 12.6 us -> 13 us
    ppermute x1, starting transfers between devices: 8.8 us -> 9.23 us  [on_device(): got_off = lax.ppermute(pay_off, AXES, off_pairs)]
    pallas_call x1, Pallas kernels: 3.46 us -> 3.03 us  [on_device(): call(remote_kernel, [SMEM] + [VMEM] * 4, [VMEM] * 2, [shape((22, CP, CP))...]
    pallas_call x1, Pallas kernels: 2.91 us -> 2.52 us  [on_device(): call(first_kernel, [SMEM, HBM, HBM], [VMEM] * 3, [shape((2 * PAY + META,...]
  transfers between devices with their start and end apart: 6 -> 6, of which waited for: 3 -> 3; matrix products, arithmetic and copies ran while one was open for 0% -> 0% of each run, Pallas kernels for 32% -> 31%
where the time goes in v4:
time: 37.9 us; the launch traced here: 37.6 us
  Pallas kernels  15.5 us (41%)
  starting transfers between devices  13 us (34%)
  waiting for transfers between devices  6.95 us (18%)
  local copies, waits for them, and re-layouts  1.4 us (4%)
  other arithmetic  0.74 us (2%)
    ppermute x1, starting transfers between devices, on_device(): got_off = lax.ppermute(pay_off, AXES, off_pairs)  9.23 us
    pallas_call x1, Pallas kernels, on_device(): call(local_kernel, [SMEM, HBM, VMEM, VMEM], [VMEM] * 4, [shape((13, CP, C...  8.46 us
    ppermute x1, waiting for transfers between devices, on_device(): got_off = lax.ppermute(pay_off, AXES, off_pairs)  3.3 us
    pallas_call x1, Pallas kernels, on_device(): call(remote_kernel, [SMEM] + [VMEM] * 4, [VMEM] * 2, [shape((22, CP, CP))...  3.03 us
    ppermute x1, starting transfers between devices, on_device(): got_roff = lax.ppermute(roff, AXES, off_pairs)  2.99 us
    pallas_call x1, Pallas kernels, on_device(): call(first_kernel, [SMEM, HBM, HBM], [VMEM] * 3, [shape((2 * PAY + META,...  2.52 us
    ppermute x1, waiting for transfers between devices, on_device(): got_roff = lax.ppermute(roff, AXES, off_pairs)  2.26 us
    pallas_call x1, Pallas kernels, on_device(): call(final_kernel, [VMEM] * 5, VMEM, shape((2, CP, BAND * CP)), [])  1.44 us
  transfers between devices with their start and end apart: 6, of which 3 were waited for; matrix products, arithmetic and copies ran while one was open for 0% of the time, Pallas kernels for 31%

profile of v4, /device:TPU:6, one launch (start us, length us, event | category | flops | bytes accessed | tf_op | source)
XLA Modules:
  0.0 37.6 jit_solution(10314967468250192148)
XLA Ops:
  0.0 0.7 %pad_add_fusion.table = s32[13,8]{1,0:T(8,128)S(1)} fusion(s32[1,8]{1,0:T(1,128)} %bitcast.6, s32[1,8]{1,0:T(1,128)} %bitcast.7, s32[3,8]{1,0:T(4,128)} %bitcast.5, s32[8,8]{1,0:T(8,128)} %param.7), kind=kLoop, calls=%fused_computation | loop fusion | flops 312 | bytes 832 | tf_op jit(solution)/shard_map/concatenate | solution.py:352
  0.7 0.0 copy-start
  0.8 1.4 %copy-done = bf16[8,3,256,128]{3,2,1,0:T(8,128)(2,1)S(1)} copy-done((bf16[8,3,256,128]{3,2,1,0:T(8,128)(2,1)S(1)}, bf16[8,3,256,128]{3,2,1,0:T(8,128)(2,1)}, u32[]{:S(2)}) %copy-start) | copy-done | bytes 1572888
  2.2 2.5 %shard_map.64 = (bf16[3088,256]{1,0:T(8,128)(2,1)S(1)}, bf16[2576,256]{1,0:T(8,128)(2,1)S(1)}, bf16[12,256,256]{2,1,0:T(8,128)(2,1)S(1)}) custom-call(s32[13,8]{1,0:T(8,128)S(1)} %pad_add_fusion.table, bf16[8,8,256,256]{3,2,1,0:T(8,128)(2,1)} %oper.3, bf16[24,256,128]{2,1,0:T(8,128)(2,1)S(1)} %bitcast.4), custom_call_target="tpu_custom_call" | custom-call | flops 1000 | bytes 1000 | tf_op jit(solution)/shard_map/pallas_call | solution.py:353
  4.7 0.1 collective-permute-start.1
  4.8 9.2 %collective-permute-start = (bf16[2576,256]{1,0:T(8,128)(2,1)S(1)}, bf16[2576,256]{1,0:T(8,128)(2,1)S(1)}, u32[]{:S(2)}, u32[]{:S(2)}) collective-permute-start(bf16[2576,256]{1,0:T(8,128)(2,1)S(1)} %get-tuple-element.16), channel_id=1, source_target_pairs={{1,2},{3,4},{5,6},{7,8},{9,10},{11,12},{13,14},{15,16},{17,18},{19... | collective-permute-start | bytes 3956744 | tf_op jit(solution)/shard_map/ppermute | solution.py:371
  14.0 0.0 collective-permute-done.1.got
  14.0 8.5 %shard_map.65 = (bf16[13,128,128]{2,1,0:T(8,128)(2,1)S(1)}, bf16[8,128,128]{2,1,0:T(8,128)(2,1)S(1)}, bf16[7,128,128]{2,1,0:T(8,128)(2,1)S(1)}, f32[22,128,128]{2,1,0:T(8,128)S(1)}) custom-call(s32[13,8]{1,0:T(8,128)S(1)} %pad_add_fusion.table, bf16[8,8,256,256]{3,2,1,0:T(8,128)(2,1)} %oper.3, bf16[3088,256]{1,0:T(8,128)(2,1)S(1)} %get-tuple-element.15.pt, ...), custom_call_target="tpu_custom_call" | custom-call | flops 1000 | bytes 1000 | tf_op jit(solution)/shard_map/pallas_call | solution.py:373
  22.5 3.0 %collective-permute-start.2 = (bf16[13,128,128]{2,1,0:T(8,128)(2,1)S(1)}, bf16[13,128,128]{2,1,0:T(8,128)(2,1)S(1)}, u32[]{:S(2)}, u32[]{:S(2)}) collective-permute-start(bf16[13,128,128]{2,1,0:T(8,128)(2,1)S(1)} %get-tuple-element.19), channel_id=1, source_target_pairs={{1,2},{3,4},{5,6},{7,8},{9,10},{11,12},{13,14},{15,16},{17,18},{19... | collective-permute-start | bytes 1277960 | tf_op jit(solution)/shard_map/ppermute | solution.py:389
  25.5 0.1 collective-permute-start.3
  25.6 0.5 %collective-permute-start.4 = (bf16[7,128,128]{2,1,0:T(8,128)(2,1)S(1)}, bf16[7,128,128]{2,1,0:T(8,128)(2,1)S(1)}, u32[]{:S(2)}, u32[]{:S(2)}) collective-permute-start(bf16[7,128,128]{2,1,0:T(8,128)(2,1)S(1)} %get-tuple-element.21), channel_id=1, source_target_pairs={{0,1},{1,0},{2,3},{3,2},{4,5},{5,4},{6,7},{7,6},{8,9},{9,8},{10,11... | collective-permute-start | bytes 688136 | tf_op jit(solution)/shard_map/ppermute | solution.py:391
  26.1 3.3 %collective-permute-done.pay = bf16[2576,256]{1,0:T(8,128)(2,1)S(1)} collective-permute-done((bf16[2576,256]{1,0:T(8,128)(2,1)S(1)}, bf16[2576,256]{1,0:T(8,128)(2,1)S(1)}, u32[]{:S(2)}, u32[]{:S(2)}) %collective-permute-start) | collective-permute-done | bytes 1318944 | tf_op jit(solution)/shard_map/ppermute | solution.py:371
  29.4 3.0 %shard_map.66 = (f32[22,128,128]{2,1,0:T(8,128)S(1)}, bf16[5,128,128]{2,1,0:T(8,128)(2,1)S(1)}) custom-call(s32[13,8]{1,0:T(8,128)S(1)} %pad_add_fusion.table, bf16[12,256,256]{2,1,0:T(8,128)(2,1)S(1)} %get-tuple-element.14.abuf, bf16[3088,256]{1,0:T(8,128)(2,1)S(1)} %get-tuple-element.15.pt, bf16[2576,256]{1,0:T(8,128)(2,1)S(1)} %collective-permute-done.pay, ...), custom_call_target="tpu_custom_call" | custom-call | flops 1000 | bytes 1000 | tf_op jit(solution)/shard_map/pallas_call | solution.py:393
  32.4 0.1 collective-permute-start.5
  32.5 1.4 %collective-permute-done.5.ron = bf16[5,128,128]{2,1,0:T(8,128)(2,1)S(1)} collective-permute-done((bf16[5,128,128]{2,1,0:T(8,128)(2,1)S(1)}, bf16[5,128,128]{2,1,0:T(8,128)(2,1)S(1)}, u32[]{:S(2)}, u32[]{:S(2)}) %collective-permute-start.5) | collective-permute-done | bytes 163872 | tf_op jit(solution)/shard_map/ppermute | solution.py:406
  33.9 0.0 collective-permute-done.4.far
  33.9 0.0 collective-permute-done.3.near
  33.9 2.3 %collective-permute-done.2.roff = bf16[13,128,128]{2,1,0:T(8,128)(2,1)S(1)} collective-permute-done((bf16[13,128,128]{2,1,0:T(8,128)(2,1)S(1)}, bf16[13,128,128]{2,1,0:T(8,128)(2,1)S(1)}, u32[]{:S(2)}, u32[]{:S(2)}) %collective-permute-start.2) | collective-permute-done | bytes 426016 | tf_op jit(solution)/shard_map/ppermute | solution.py:389
  36.2 1.4 %shard_map.67 = f32[2,128,1408]{2,1,0:T(8,128)} custom-call(f32[22,128,128]{2,1,0:T(8,128)S(1)} %get-tuple-element.18.own, bf16[13,128,128]{2,1,0:T(8,128)(2,1)S(1)} %collective-permute-done.2.roff, bf16[8,128,128]{2,1,0:T(8,128)(2,1)S(1)} %collective-permute-done.3.near, bf16[7,128,128]{2,1,0:T(8,128)(2,1)S(1)} %collective-permute-done.4.far, ...), custom_call_target="tpu_custom_call" | custom-call | flops 1000 | bytes 1000 | tf_op jit(solution)/shard_map/pallas_call | solution.py:408
Async XLA Ops:
  0.7 1.4 %copy-start = (bf16[8,3,256,128]{3,2,1,0:T(8,128)(2,1)S(1)}, bf16[8,3,256,128]{3,2,1,0:T(8,128)(2,1)}, u32[]{:S(2)}) copy-start(bf16[8,3,256,128]{3,2,1,0:T(8,128)(2,1)} %param.9) | copy-start | bytes 4718596
  4.7 9.3 %collective-permute-start.1 = (bf16[3088,256]{1,0:T(8,128)(2,1)S(1)}, bf16[3088,256]{1,0:T(8,128)(2,1)S(1)}, u32[]{:S(2)}, u32[]{:S(2)}) collective-permute-start(bf16[3088,256]{1,0:T(8,128)(2,1)S(1)} %get-tuple-element.15.pt), channel_id=1, source_target_pairs={{0,1},{1,0},{2,3},{3,2},{4,5},{5,4},{6,7},{7,6},{8,9},{9,8},{10,11... | collective-permute-start | bytes 4743176 | tf_op jit(solution)/shard_map/ppermute | solution.py:370
  4.8 24.6 %collective-permute-start = (bf16[2576,256]{1,0:T(8,128)(2,1)S(1)}, bf16[2576,256]{1,0:T(8,128)(2,1)S(1)}, u32[]{:S(2)}, u32[]{:S(2)}) collective-permute-start(bf16[2576,256]{1,0:T(8,128)(2,1)S(1)} %get-tuple-element.16), channel_id=1, source_target_pairs={{1,2},{3,4},{5,6},{7,8},{9,10},{11,12},{13,14},{15,16},{17,18},{19... | collective-permute-start | bytes 3956744 | tf_op jit(solution)/shard_map/ppermute | solution.py:371
  22.5 13.7 %collective-permute-start.2 = (bf16[13,128,128]{2,1,0:T(8,128)(2,1)S(1)}, bf16[13,128,128]{2,1,0:T(8,128)(2,1)S(1)}, u32[]{:S(2)}, u32[]{:S(2)}) collective-permute-start(bf16[13,128,128]{2,1,0:T(8,128)(2,1)S(1)} %get-tuple-element.19), channel_id=1, source_target_pairs={{1,2},{3,4},{5,6},{7,8},{9,10},{11,12},{13,14},{15,16},{17,18},{19... | collective-permute-start | bytes 1277960 | tf_op jit(solution)/shard_map/ppermute | solution.py:389
  25.5 8.4 %collective-permute-start.3 = (bf16[8,128,128]{2,1,0:T(8,128)(2,1)S(1)}, bf16[8,128,128]{2,1,0:T(8,128)(2,1)S(1)}, u32[]{:S(2)}, u32[]{:S(2)}) collective-permute-start(bf16[8,128,128]{2,1,0:T(8,128)(2,1)S(1)} %get-tuple-element.20), channel_id=1, source_target_pairs={{0,1},{1,0},{2,3},{3,2},{4,5},{5,4},{6,7},{7,6},{8,9},{9,8},{10,11... | collective-permute-start | bytes 786440 | tf_op jit(solution)/shard_map/ppermute | solution.py:390
  25.6 8.3 %collective-permute-start.4 = (bf16[7,128,128]{2,1,0:T(8,128)(2,1)S(1)}, bf16[7,128,128]{2,1,0:T(8,128)(2,1)S(1)}, u32[]{:S(2)}, u32[]{:S(2)}) collective-permute-start(bf16[7,128,128]{2,1,0:T(8,128)(2,1)S(1)} %get-tuple-element.21), channel_id=1, source_target_pairs={{0,1},{1,0},{2,3},{3,2},{4,5},{5,4},{6,7},{7,6},{8,9},{9,8},{10,11... | collective-permute-start | bytes 688136 | tf_op jit(solution)/shard_map/ppermute | solution.py:391
  32.4 1.5 %collective-permute-start.5 = (bf16[5,128,128]{2,1,0:T(8,128)(2,1)S(1)}, bf16[5,128,128]{2,1,0:T(8,128)(2,1)S(1)}, u32[]{:S(2)}, u32[]{:S(2)}) collective-permute-start(bf16[5,128,128]{2,1,0:T(8,128)(2,1)S(1)} %get-tuple-element.22), channel_id=1, source_target_pairs={{0,1},{1,0},{2,3},{3,2},{4,5},{5,4},{6,7},{7,6},{8,9},{9,8},{10,11... | collective-permute-start | bytes 491528 | tf_op jit(solution)/shard_map/ppermute | solution.py:406
